TPU v7x, 128 devices: a whole 4x4x4 slice. The times are simulated.
128 devices in a mesh: section: 8 (over x_lo, z), tensor: 16 (over y, x_hi, core).
Axes of the slice: x: 4 (x_hi: 2, x_lo: 2; x = x_hi * 2 + x_lo), y: 4, z: 4, core: 2. Of those that a mesh axis runs over, the one named last changes fastest.
Arguments:
- hidden_in: bfloat16 [8, 1024, 8192], P('section', 'tensor'), may hold values from -6 to 6
- norm_gain: bfloat16 [8, 8192], P('section'), may hold values from 0.5 to 1.5
- w_query: bfloat16 [8, 8192, 8192], P('section', None, 'tensor')
- bias_query: bfloat16 [8, 8192], P('section', 'tensor'), may hold values from -3 to 3
- w_key: bfloat16 [8, 8192, 1024], P('section', 'tensor')
- w_value: bfloat16 [8, 8192, 1024], P('section', 'tensor'), may hold values from -0.0625 to 0.0625
- bias_value: bfloat16 [8, 1024], P('section'), may hold values from -3 to 3
- w_out: bfloat16 [8, 8192, 8192], P('section', 'tensor'), may hold values from -0.0625 to 0.0625
- visible_end: int32 [8, 1024], P('section'), may hold values from 1 to 1024, as said below
Outputs:
- handed: bfloat16 [8, 1024, 8192], P('section', 'tensor')
Inputs may be any that keep to these rules, and one draw needn't show every extreme that they name: Token i attends keys j < visible_end[s, i]; visible_end[s, i] >= i + 1; the tokens of one frame segment share the end of their segment, an instruction token i has i + 1, and the last token has 1024.
All inputs are finite; a program needn't handle non-finite values.
Results may differ from a plain program's by a relative error of at most 0.015.
Values may be sent and summed in bfloat16 or wider, within the bound.
A program may use at most 128 MiB of HBM per device.

v0:
```python
import jax
import jax.numpy as jnp
from jax import lax
from jax.sharding import PartitionSpec as P

KV = 8
HEAD = 128


def from_behind(array, axis, by):
    count = lax.axis_size(axis)
    return lax.ppermute(array, axis, [(i, (i + by) % count) for i in range(count)])


def normalize(rows, gain):
    values = rows.astype(jnp.float32)
    power = jnp.mean(values * values, axis=-1, keepdims=True)
    return (values * lax.rsqrt(power + 1e-06) * gain.astype(jnp.float32)).astype(jnp.bfloat16)


def on_device(
    hidden_in, norm_gain, w_query, bias_query, w_key, w_value, bias_value, w_out, visible_end
):
    rows = hidden_in[0]
    gain = norm_gain[0]
    count = lax.axis_size("tensor")
    place = lax.axis_index("tensor")
    repeat = count // KV
    owner = place // repeat
    normed = normalize(lax.all_gather(rows, "tensor", axis=0, tiled=True), gain)
    total = normed.shape[0]
    local_width = w_query.shape[2]
    local_heads = local_width // HEAD
    query = (
        jnp.dot(normed, w_query[0], preferred_element_type=jnp.float32)
        + bias_query[0].astype(jnp.float32)
    ).astype(jnp.bfloat16)
    width_rows = w_key.shape[1]
    stacked = jnp.stack([w_key[0], w_value[0]], axis=1).reshape(width_rows, 2, KV, HEAD)
    spread = jnp.repeat(stacked, repeat, axis=2)
    mine = lax.all_to_all(spread, "tensor", split_axis=2, concat_axis=0, tiled=True)
    key_float = jnp.dot(normed, mine[:, 0, 0, :], preferred_element_type=jnp.float32)
    value_float = jnp.dot(normed, mine[:, 1, 0, :], preferred_element_type=jnp.float32)
    value_bias = lax.dynamic_slice_in_dim(bias_value[0], owner * HEAD, HEAD, 0).astype(jnp.float32)
    keys = key_float.astype(jnp.bfloat16)
    values = (value_float + value_bias).astype(jnp.bfloat16)
    query_heads = query.reshape(total, local_heads, HEAD)
    scores = jnp.einsum("thd,sd->hts", query_heads, keys, preferred_element_type=jnp.float32) * (
        1.0 / HEAD**0.5
    )
    visible = jnp.arange(total, dtype=jnp.int32)[None, :] < visible_end[0][:, None]
    scores = jnp.where(visible[None, :, :], scores, -1e30)
    top = jnp.max(scores, axis=-1, keepdims=True)
    expo = jnp.exp(scores - top)
    weights = (expo / jnp.sum(expo, axis=-1, keepdims=True)).astype(jnp.bfloat16)
    context = jnp.einsum("hts,sd->thd", weights, values, preferred_element_type=jnp.float32).astype(
        jnp.bfloat16
    )
    context = context.reshape(total, local_width)
    out_rows = w_out[0]
    attended = lax.psum_scatter(
        jnp.dot(context, out_rows, preferred_element_type=jnp.float32).astype(jnp.bfloat16),
        "tensor",
        scatter_dimension=0,
        tiled=True,
    ).astype(jnp.float32)
    layer_out = (rows.astype(jnp.float32) + attended).astype(jnp.bfloat16)
    handed = from_behind(layer_out, "section", 1)
    return handed[None]


def solution(mesh):
    placed = (
        P("section", "tensor", None),
        P("section", None),
        P("section", None, "tensor"),
        P("section", "tensor"),
        P("section", "tensor", None),
        P("section", "tensor", None),
        P("section", None),
        P("section", "tensor", None),
        P("section", None),
    )
    return jax.shard_map(
        on_device,
        mesh=mesh,
        in_specs=placed,
        out_specs=P("section", "tensor", None),
        check_vma=False,
    )
```

profile of v0, /device:TPU:0, one launch (start us, length us, event | category | flops | bytes accessed | tf_op | source)
XLA Modules:
  0.0 423.4 jit_solution(9547044784517909046)
XLA Ops:
  6.5 0.0 copy-start.4
  6.5 0.0 copy-start.6
  6.5 0.0 copy-start.5
  6.5 0.0 all-gather.3.cloned.1.call-start
  6.5 0.7 all-gather.3.cloned.1.call-update
  7.3 1.5 copy.26
  8.8 1.5 copy.25
  10.3 0.2 pad_maximum_fusion
  10.5 0.4 copy.16
  10.9 2.9 broadcast_in_dim.16
  13.8 7.2 %all-to-all-start = ((bf16[512,2,16,128]{3,0,1,2:T(8,128)(2,1)}), bf16[512,2,16,128]{3,0,1,2:T(8,128)(2,1)}, u32[]{:S(2)}, u32[]{:S(2)}) async-start(bf16[512,2,16,128]{3,0,1,2:T(8,128)(2,1)} %bitcast.85), calls=%async_computation | async-start | bytes 8388608 | tf_op jit(solution)/shard_map/all_to_all | solution.py:41
  21.0 0.0 reduce-scatter.2.cloned.1.call-start
  21.0 0.0 copy-done.4
  21.1 0.0 copy-done.6
  21.1 0.7 bitcast_convert_fusion
  21.8 0.0 copy-done.5
  21.8 0.8 iota_compare_fusion
  22.6 64.4 %all-to-all-done = bf16[512,2,16,128]{3,0,1,2:T(8,128)(2,1)} async-done(((bf16[512,2,16,128]{3,0,1,2:T(8,128)(2,1)}), bf16[512,2,16,128]{3,0,1,2:T(8,128)(2,1)}, u32[]{:S(2)}, u32[]{:S(2)}) %all-to-all-start) | async-done | bytes 4194336 | tf_op jit(solution)/shard_map/all_to_all | solution.py:41
  87.0 4.7 %copy.17 = bf16[512,2,16,128]{3,0,2,1:T(8,128)(2,1)} copy(bf16[512,2,16,128]{3,0,1,2:T(8,128)(2,1)} %all-to-all-done) | data formatting | bytes 8388608 | tf_op jit(solution)/shard_map/all_to_all | solution.py:41
  91.7 70.4 %all-gather.3.cloned.1.call-done = bf16[1,1024,8192]{2,1,0:T(8,128)(2,1)} async-done(((bf16[1,64,8192]{2,1,0:T(8,128)(2,1)}), bf16[1,1024,8192]{2,1,0:T(8,128)(2,1)}) %all-gather.3.cloned.1.call-update) | async-done | bytes 16777232 | tf_op jit(solution)/shard_map/all_gather | solution.py:30
  162.2 0.0 copy-start
  162.2 7.5 %fusion.1 = f32[1024]{0:T(1024)S(1)} fusion(bf16[1,1024,8192]{2,1,0:T(8,128)(2,1)} %all-gather.3.cloned.1.call-done), kind=kLoop, calls=%fused_computation.3 | loop fusion | flops 25164800 | bytes 16781312 | tf_op jit(solution)/shard_map/reduce_sum | solution.py:17
  169.7 3.2 copy-done
  172.8 0.0 copy-start.3
  172.8 4.7 %fusion.3 = bf16[1024,8192]{1,0:T(8,128)(2,1)S(1)} fusion(bf16[1,1024,8192]{2,1,0:T(8,128)(2,1)S(1)} %copy-done, f32[8192]{0:T(1024)S(1)} %bitcast.93, f32[1024]{0:T(1024)S(1)} %add_rsqrt_fusion), kind=kLoop, calls=%fused_computation.5 | loop fusion | flops 33554432 | bytes 33591296 | tf_op jit(solution)/shard_map/convert_element_type | solution.py:18
  177.6 0.0 copy-start.1
  177.6 5.7 %copy-done.1 = bf16[1024,8192]{1,0:T(8,128)(2,1)} copy-done((bf16[1024,8192]{1,0:T(8,128)(2,1)}, bf16[1024,8192]{1,0:T(8,128)(2,1)S(1)}, u32[]{:S(2)}) %copy-start.1) | copy-done | bytes 16777240
  183.3 0.0 copy-done.3
  183.3 4.5 %fusion.24 = bf16[1024,128,1]{1,0,2:T(8,128)(2,1)S(1)} fusion(bf16[1024,8192]{1,0:T(8,128)(2,1)S(1)} %fusion.3, bf16[8192,2,1,128]{3,0,1,2:T(8,128)(2,1)S(1)} %bitcast.87), kind=kOutput, calls=%fused_computation.33 | convolution fusion | flops 2147614720 | bytes 19136512 | tf_op jit(solution)/shard_map/dot_general | solution.py:42
  187.8 14.9 %add_convert_fusion = bf16[1024,512]{0,1:T(8,128)(2,1)S(1)} fusion(bf16[1024,8192]{1,0:T(8,128)(2,1)} %copy-done.1, bf16[1,8192,512]{2,1,0:T(8,128)(2,1)} %param.11, f32[512]{0:T(512)S(1)} %bitcast.95), kind=kOutput, calls=%fused_computation.26 | convolution fusion | flops 8590983168 | bytes 26216448 | tf_op jit(solution)/shard_map/dot_general | solution.py:35
  202.7 9.6 %fusion.28 = (f32[4,1024]{1,0:T(4,128)S(1)}, f32[4,1024,1024]{1,2,0:T(8,128)}) fusion(pred[1024,1024]{0,1:T(8,128)(4,1)S(1)} %iota_compare_fusion, bf16[1024,128,1]{1,0,2:T(8,128)(2,1)S(1)} %fusion.24, bf16[1024,4,128]{0,2,1:T(8,128)(2,1)S(1)} %bitcast.96), kind=kOutput, calls=%fused_computation.39 | convolution fusion | flops 1090520064 | bytes 19152896 | tf_op jit(solution)/shard_map/sub | solution.py:54
  212.3 14.4 %fusion.19 = bf16[128,4,1024]{2,0,1:T(8,128)(2,1)S(1)} fusion(f32[4,1024,1024]{1,2,0:T(8,128)} %get-tuple-element.6, f32[4,1024]{1,0:T(4,128)S(1)} %get-tuple-element.5, bf16[1024,8192]{1,0:T(8,128)(2,1)} %copy-done.1, bf16[8192,2,1,128]{3,0,1,2:T(8,128)(2,1)} %bitcast.86, f32[128]{0:T(128)S(1)} %bitcast_convert_fusion), kind=kOutput, calls=%fused_computation.28 | convolution fusion | flops 3230400512 | bytes 36717056 | tf_op jit(solution)/shard_map/hts,sd->thd/dot_general | solution.py:56
  226.7 0.0 copy-start.2
  226.7 15.8 %convolution_convert_fusion = bf16[1024,8192]{1,0:T(8,128)(2,1)} fusion(bf16[1024,512]{0,1:T(8,128)(2,1)S(1)} %bitcast.97, bf16[1,512,8192]{2,1,0:T(8,128)(2,1)} %param.16), kind=kOutput, calls=%fused_computation.9 | convolution fusion | flops 8598323200 | bytes 26214400 | tf_op jit(solution)/shard_map/dot_general | solution.py:62
  242.6 0.0 reduce-scatter.2.cloned.1.call-update
  242.6 145.1 %reduce-scatter.2.cloned.1.call-done = bf16[64,8192]{1,0:T(8,128)(2,1)} async-done(((bf16[1024,8192]{1,0:T(8,128)(2,1)}), bf16[64,8192]{1,0:T(8,128)(2,1)}) %reduce-scatter.2.cloned.1.call-update) | async-done | bytes 1048592 | tf_op jit(solution)/shard_map/reduce_scatter | solution.py:61
  387.7 0.0 copy-done.2
  387.7 1.5 fusion.14
  389.1 1.6 collective-permute-start
  390.8 24.8 %collective-permute-done = bf16[64,8192]{1,0:T(8,128)(2,1)S(1)} collective-permute-done((bf16[64,8192]{1,0:T(8,128)(2,1)S(1)}, bf16[64,8192]{1,0:T(8,128)(2,1)S(1)}, u32[]{:S(2)}, u32[]{:S(2)}) %collective-permute-start) | collective-permute-done | bytes 1048608 | tf_op jit(solution)/shard_map/ppermute | solution.py:12
  415.6 1.0 copy.28
  (3 shorter events, 0.0 us)
Async XLA Ops:
  6.5 14.5 %copy-start.4 = (bf16[1,8192]{1,0:T(2,128)(2,1)S(1)}, bf16[1,8192]{1,0:T(2,128)(2,1)}, u32[]{:S(2)}) copy-start(bf16[1,8192]{1,0:T(2,128)(2,1)} %param.10) | copy-start | bytes 49156
  6.5 14.5 %copy-start.6 = (bf16[1,512]{1,0:T(2,128)(2,1)S(1)}, bf16[1,512]{1,0:T(2,128)(2,1)}, u32[]{:S(2)}) copy-start(bf16[1,512]{1,0:T(2,128)(2,1)} %param.12) | copy-start | bytes 3076
  6.5 15.3 %copy-start.5 = (s32[1,1024]{1,0:T(1,128)S(1)}, s32[1,1024]{1,0:T(1,128)}, u32[]{:S(2)}) copy-start(s32[1,1024]{1,0:T(1,128)} %param.17) | copy-start | bytes 12292
  6.5 155.6 %all-gather.3.cloned.1.call-start = ((), (), s32[]{:S(2)}) async-start(), calls=%async_computation.3 | async-start | bytes 17825792 | tf_op jit(solution)/shard_map/all_gather | solution.py:30
  13.8 73.2 %all-to-all-start = ((bf16[512,2,16,128]{3,0,1,2:T(8,128)(2,1)}), bf16[512,2,16,128]{3,0,1,2:T(8,128)(2,1)}, u32[]{:S(2)}, u32[]{:S(2)}) async-start(bf16[512,2,16,128]{3,0,1,2:T(8,128)(2,1)} %bitcast.85), calls=%async_computation | async-start | bytes 8388608 | tf_op jit(solution)/shard_map/all_to_all | solution.py:41
  21.0 366.7 %reduce-scatter.2.cloned.1.call-start = ((), (), s32[]{:S(2)}) async-start(), calls=%async_computation.2 | async-start | bytes 17825792 | tf_op jit(solution)/shard_map/reduce_scatter | solution.py:61
  162.2 10.7 %copy-start = (bf16[1,1024,8192]{2,1,0:T(8,128)(2,1)S(1)}, bf16[1,1024,8192]{2,1,0:T(8,128)(2,1)}, u32[]{:S(2)}) copy-start(bf16[1,1024,8192]{2,1,0:T(8,128)(2,1)} %all-gather.3.cloned.1.call-done) | copy-start | bytes 50331652
  172.8 10.5 %copy-start.3 = (bf16[512,2,16,128]{3,0,2,1:T(8,128)(2,1)S(1)}, bf16[512,2,16,128]{3,0,2,1:T(8,128)(2,1)}, u32[]{:S(2)}) copy-start(bf16[512,2,16,128]{3,0,2,1:T(8,128)(2,1)} %copy.17) | copy-start | bytes 12582916
  177.6 5.7 %copy-start.1 = (bf16[1024,8192]{1,0:T(8,128)(2,1)}, bf16[1024,8192]{1,0:T(8,128)(2,1)S(1)}, u32[]{:S(2)}) copy-start(bf16[1024,8192]{1,0:T(8,128)(2,1)S(1)} %fusion.3) | copy-start | bytes 50331652
  226.7 161.0 %copy-start.2 = (bf16[1,64,8192]{2,1,0:T(8,128)(2,1)S(1)}, bf16[1,64,8192]{2,1,0:T(8,128)(2,1)}, u32[]{:S(2)}) copy-start(bf16[1,64,8192]{2,1,0:T(8,128)(2,1)} %param.9) | copy-start | bytes 3145732
  389.1 26.5 %collective-permute-start = (bf16[64,8192]{1,0:T(8,128)(2,1)S(1)}, bf16[64,8192]{1,0:T(8,128)(2,1)S(1)}, u32[]{:S(2)}, u32[]{:S(2)}) collective-permute-start(bf16[64,8192]{1,0:T(8,128)(2,1)S(1)} %fusion.14), channel_id=1, source_target_pairs={{0,16},{16,32},{32,48},{48,64},{64,80},{80,96},{96,112},{112,0},{1... | collective-permute-start | bytes 3145736 | tf_op jit(solution)/shard_map/ppermute | solution.py:12
Sparse Core Ops, SparseCore 0:
  9.8 152.2 all-gather.2
  242.7 144.8 reduce-scatter.1
where the time goes:
time: 424 us; the launch traced here: 423 us
  waiting for transfers between devices  306 us (72%)
  matrix products  59.2 us (14%)
  local copies, waits for them, and re-layouts  20.9 us (5%)
  other arithmetic  15.4 us (4%)
  between operations  13.6 us (3%)
  starting transfers between devices  8.84 us (2%)
    reduce_scatter x1, waiting for transfers between devices, on_device(): lax.psum_scatter(jnp.dot(context, out_rows, preferred_element_type=jnp.fl...  145 us
    all_gather x1, waiting for transfers between devices, on_device(): normed = normalize(lax.all_gather(rows, 'tensor', axis=0, tiled=True), gain)  70.4 us
    all_to_all x1, waiting for transfers between devices, on_device(): lax.all_to_all(spread, 'tensor', split_axis=2, concat_axis=0, tiled=True)  64.4 us
    ppermute x1, waiting for transfers between devices, from_behind(): lax.ppermute(array, axis, [(i, (i + by) % count) for i in range(count)])  24.8 us
    dot_general x1, matrix products, on_device(): jnp.dot(context, out_rows, preferred_element_type=jnp.float32)  15.8 us
    dot_general x1, matrix products, on_device(): jnp.dot(normed, w_query[0], preferred_element_type=jnp.float32)  14.9 us
    dot_general x1, matrix products, on_device(): jnp.einsum('hts,sd->thd', weights, values, preferred_element_type=jnp.flo...  14.4 us
    unnamed x17, local copies, waits for them, and re-layouts  12.8 us
  transfers between devices with their start and end apart: 4, of which 4 were waited for; matrix products, arithmetic and copies ran while one was open for 3% of the time, Pallas kernels for 0%

commit v1 on v0

v1 whole, which is shorter than its diff:
```python
import jax
import jax.numpy as jnp
from jax import lax
from jax.experimental import pallas as pl
from jax.experimental.pallas import tpu as pltpu
from jax.sharding import PartitionSpec as P

MESH = pl.DeviceIdType.MESH
BF = jnp.bfloat16
F32 = jnp.float32
HEAD = 128
AHEAD = 3
SKEW = 2
GATHER_ACROSS = 3
LOG2E = 1.4426950408889634


def across(chunk):
    return lax.rem(chunk, 8) == 5


def mo(value, by):
    return pl.multiple_of(value, by)


def layer(
    hid, gain, wq, bq, wk, wv, bv, wo, ends, out,
    G, WQ, WKV, WO, ACC, ACCKV, Q, KV, CTX, BQ, E, KID, STG,
    ag_s, ag_r, rs_s, rs_r, ho_s, ho_r, kvw_s, kvw_r, own_kv, fw_s, fw_r,
    wq_l, wq_s, wq_r, wo_l, wo_s, wo_r, bq_s, bq_r, kv_s, kv_r, free,
):
    section = lax.axis_index("section")
    place = lax.axis_index("tensor")
    y, h, c = lax.div(place, 4), lax.rem(lax.div(place, 2), 2), lax.rem(place, 2)
    chip = lax.div(place, 2)

    def block(dy, flip):
        return lax.rem(y + dy, 4) * 2 + (1 - h if flip else h)

    def peer(dy, flip):
        return block(dy, flip) * 2 + c

    yp, ym, xx = peer(1, 0), peer(3, 0), peer(0, 1)
    other = chip * 2 + (1 - c)
    own = chip
    nxt, prv = lax.rem(section + 1, 8), lax.rem(section + 7, 8)

    def send(src, dst, ss, rs, to):
        return pltpu.make_async_remote_copy(
            src_ref=src, dst_ref=dst, send_sem=ss, recv_sem=rs,
            device_id={"tensor": to}, device_id_type=MESH,
        )

    def wq_local(j):
        return pltpu.make_async_copy(
            wq.at[0, pl.ds(mo(j * 1024, 1024), 1024), :],
            WQ.at[j, :, pl.ds(mo(c * 512, 512), 512)],
            wq_l.at[j],
        )

    def wo_local(q):
        return pltpu.make_async_copy(
            wo.at[0, :, pl.ds(mo(q * 2048, 2048), 2048)],
            WO.at[q, pl.ds(mo(c * 512, 512), 512), :],
            wo_l.at[q],
        )

    def kv_local(w, n):
        return pltpu.make_async_copy(
            w.at[0, :, pl.ds(mo(chip * HEAD, HEAD), HEAD)],
            WKV.at[chip, pl.ds(mo(c * 512, 512), 512), n * HEAD : (n + 1) * HEAD],
            own_kv.at[n],
        )

    def wq_push(j):
        return send(
            wq.at[0, pl.ds(mo(j * 1024, 1024), 1024), :],
            WQ.at[j, :, pl.ds(mo(c * 512, 512), 512)],
            wq_s.at[j], wq_r.at[j], other,
        )

    def wo_push(q):
        return send(
            wo.at[0, :, pl.ds(mo(q * 2048, 2048), 2048)],
            WO.at[q, pl.ds(mo(c * 512, 512), 512), :],
            wo_s.at[q], wo_r.at[q], other,
        )

    def kvw(w, n, d):
        to = lax.rem(chip + d, 8)
        return send(
            w.at[0, :, pl.ds(mo(to * HEAD, HEAD), HEAD)],
            WKV.at[chip, pl.ds(mo(c * 512, 512), 512), n * HEAD : (n + 1) * HEAD],
            kvw_s.at[n, d], kvw_r.at[n, d], to * 2 + c,
        )

    def forward(d):
        came = lax.rem(chip + 8 - d, 8)
        part = WKV.at[came, pl.ds(mo(c * 512, 512), 512), :]
        return send(part, part, fw_s.at[d], fw_r.at[d], other)

    def gather(kind, j):
        side = j == GATHER_ACROSS
        if kind == 0:
            b, lo, n, to = own, 0, 64, yp
        elif kind == 1:
            b, lo, n, to = own, 0, 64, ym
        elif kind == 2:
            b, lo, n, to = own, 0, 64, xx
        elif kind == 3:
            b, lo, n = jnp.where(side, block(3, 0), block(0, 1)), 0, 64
            to = jnp.where(side, xx, yp)
        elif kind == 4:
            b, lo, n = jnp.where(side, block(1, 0), block(0, 1)), 0, 64
            to = jnp.where(side, xx, ym)
        elif kind == 5:
            b, lo, n, to = block(3, 0), 0, 32, yp
        elif kind == 6:
            b, lo, n, to = block(1, 0), 32, 32, ym
        else:
            b, lo, n, to = block(2, 0), 0, 64, xx
        part = G.at[j, pl.ds(mo(b * 64 + lo, 32), n), :]
        return send(part, part, ag_s.at[kind, j], ag_r.at[kind, j], to)

    def gathered(kind, j):
        b = (block(3, 0), block(1, 0), block(0, 1), block(3, 1), block(1, 1),
             block(2, 0), block(2, 0), block(2, 1))[kind]
        lo = 32 if kind == 6 else 0
        n = 32 if kind in (5, 6) else 64
        part = G.at[j, pl.ds(mo(b * 64 + lo, 32), n), :]
        send(part, part, ag_s.at[kind, j], ag_r.at[kind, j], xx).wait_recv()

    def term(k, b, half=0):
        return lax.div(k, 4), mo(lax.rem(k, 4) * 256 + b * 32 + half * 16, 16)

    def slot(k, n, half=0):
        return lax.div(k, 2), mo(lax.rem(k, 2) * 256 + n * 32 + half * 16, 16)

    def reduce(kind, k):
        side = across(k)
        half, rows, into, at = 0, 32, kind, 0
        if kind == 0:
            b, to = block(3, 0), ym
        elif kind == 1:
            b, to = block(1, 0), yp
        elif kind == 2:
            b, to = block(0, 1), xx
        elif kind == 3:
            b, to = block(3, 1), jnp.where(side, xx, ym)
        elif kind == 4:
            b, to = block(1, 1), jnp.where(side, xx, yp)
        elif kind == 5:
            b, to, rows = block(2, 0), ym, 16
        elif kind == 6:
            b, to, rows, half, into, at = block(2, 0), yp, 16, 1, 5, 1
        else:
            b, to, into = block(2, 1), xx, 6
        i, row = term(k, b, half)
        o, line = slot(k, into, at)
        return send(
            WQ.at[i, pl.ds(row, rows), :], G.at[o, pl.ds(line, rows), :],
            rs_s.at[kind, k], rs_r.at[kind, k], to,
        )

    def add(k, b, half, arrived):
        i, row = term(k, b, half)
        total = WQ[i, pl.ds(row, 16), :].astype(F32)
        for n, at in arrived:
            o, line = slot(k, n, at)
            total = total + G[o, pl.ds(line, 16), :].astype(F32)
        return total, i, row

    def add_in(k, b, half, arrived):
        total, i, row = add(k, b, half, arrived)
        WQ[i, pl.ds(row, 16), :] = total.astype(BF)

    def hand(k):
        r, q = lax.div(k, 4), lax.rem(k, 4)
        rows, columns = pl.ds(mo(r * 16, 16), 16), pl.ds(mo(q * 2048, 2048), 2048)
        return pltpu.make_async_remote_copy(
            src_ref=STG.at[rows, columns], dst_ref=out.at[0, rows, columns],
            send_sem=ho_s.at[k], recv_sem=ho_r.at[k],
            device_id={"section": nxt}, device_id_type=MESH,
        )

    for n, w in enumerate((wk, wv)):
        kv_local(w, n).start()
    for j in range(8):
        wq_local(j).start()
    for q in range(4):
        wo_local(q).start()

    barrier = pltpu.get_barrier_semaphore()
    for d in range(1, 8):
        pl.semaphore_signal(
            barrier, inc=1, device_id={"tensor": lax.rem(chip + d, 8) * 2 + c}, device_id_type=MESH
        )
    pl.semaphore_signal(barrier, inc=1, device_id={"tensor": other}, device_id_type=MESH)
    pl.semaphore_signal(barrier, inc=1, device_id={"section": prv}, device_id_type=MESH)
    pl.semaphore_wait(barrier, 9)

    for d in (4, 3, 5, 2, 6, 1, 7):
        for n, w in enumerate((wk, wv)):
            kvw(w, n, d).start()

    def norm_rows(rg, carry):
        rows = hid[0, pl.ds(mo(rg * 16, 16), 16), :].astype(F32)
        power = jnp.mean(rows * rows, axis=-1, keepdims=True)
        scale = lax.rsqrt(power + 1e-06)
        normed = (rows * scale * gain[...].astype(F32)).astype(BF)
        for j in range(8):
            G[j, pl.ds(mo(own * 64 + rg * 16, 16), 16), :] = normed[:, j * 1024 : (j + 1) * 1024]
        return carry

    lax.fori_loop(0, 4, norm_rows, 0)
    for j in range(AHEAD):
        for kind in range(3):
            gather(kind, j).start()
    BQ[c] = jnp.broadcast_to(bq[...], (16, 512))
    bias_push = send(BQ.at[c], BQ.at[c], bq_s.at[0], bq_r.at[0], other)
    bias_push.start()
    for j in range(8):
        wq_push(j).start()
    for q in range(4):
        wo_push(q).start()
    ACC[...] = jnp.zeros_like(ACC)
    ACCKV[...] = jnp.zeros_like(ACCKV)
    for b in range(8):
        line = jnp.broadcast_to(ends[:, b * 128 : (b + 1) * 128].astype(F32), (128, 128))
        E[b] = line.T
    lane = lax.broadcasted_iota(jnp.int32, (8, 512), 1)
    token = lane + lax.div(lane, 64) * 64
    KID[:, 0:512] = token.astype(F32)
    KID[:, 512:1024] = (token + 64).astype(F32)
    KV[:, 256:384] = jnp.ones((1024, 128), BF)

    def kv_stage(j, carry):
        ACCKV[...] += jnp.dot(G[j], WKV[j], preferred_element_type=F32)
        return carry

    def gather_step(i, carry):
        @pl.when(i < 8 - AHEAD)
        def _():
            for kind in range(3):
                gather(kind, i + AHEAD).start()

        @pl.when(i < 8)
        def _():
            gathered(0, i)
            gather(5, i).start()
            gathered(1, i)
            gather(6, i).start()
            gathered(2, i)
            gather(3, i).start()
            gather(4, i).start()

        @pl.when(i == 0)
        def _():
            for n, w in enumerate((wk, wv)):
                kv_local(w, n).wait()
            forward(0).start()

        @pl.when((i >= 1) & (i < 8))
        def _():
            for n, w in enumerate((wk, wv)):
                came = lax.rem(chip + 8 - i, 8)
                part = WKV.at[came, pl.ds(mo(c * 512, 512), 512), n * HEAD : (n + 1) * HEAD]
                send(part, part, kvw_s.at[n, i], kvw_r.at[n, i], other).wait_recv()
            forward(i).start()

        @pl.when((i >= 1) & (i < 9))
        def _():
            gathered(5, i - 1)
            gathered(6, i - 1)
            gather(7, i - 1).start()

        @pl.when(i >= 3)
        def _():
            j = i - 3
            gathered(3, j)
            gathered(4, j)
            gathered(7, j)

            @pl.when(i == 8)
            def _():
                for d in range(8):
                    came = lax.rem(chip + 8 - d, 8)
                    part = WKV.at[came, pl.ds(mo((1 - c) * 512, 512), 512), :]
                    send(part, part, fw_s.at[d], fw_r.at[d], other).wait_recv()

            @pl.when(i >= 8)
            def _():
                lax.fori_loop((i - 8) * 3, jnp.minimum((i - 8) * 3 + 3, 8), kv_stage, 0)

            @pl.when(i == 10)
            def _():
                total = ACCKV[...]
                rows = pl.ds(mo(c * 512, 512), 512)
                KV[rows, 0:HEAD] = total[:, 0:HEAD].astype(BF)
                bias = bv[:, pl.ds(mo(chip * HEAD, HEAD), HEAD)].astype(F32)
                KV[rows, HEAD : 2 * HEAD] = (total[:, HEAD:] + bias).astype(BF)
                part = KV.at[rows, 0 : 2 * HEAD]
                send(part, part, kv_s.at[0], kv_r.at[0], other).start()

            wq_local(j).wait()
            part = WQ.at[j, :, pl.ds(mo((1 - c) * 512, 512), 512)]
            send(part, part, wq_s.at[j], wq_r.at[j], other).wait_recv()
            for n in range(2):
                columns = slice(n * 512, (n + 1) * 512)
                ACC[:, columns] += jnp.dot(G[j], WQ[j, :, columns], preferred_element_type=F32)

        return carry

    lax.fori_loop(0, 11, gather_step, 0)

    send(BQ.at[1 - c], BQ.at[1 - c], bq_s.at[0], bq_r.at[0], other).wait_recv()
    for n in range(2):
        for b in range(8):
            Q[b, :, n * 512 : (n + 1) * 512] = (
                ACC[b * 64 : (b + 1) * 64, n * 512 : (n + 1) * 512] + BQ[n, 0:1, :].astype(F32)
            ).astype(BF)

    def gather_sent(j, carry):
        for kind in range(8):
            gather(kind, j).wait_send()
        return carry

    lax.fori_loop(0, 8, gather_sent, 0)
    for to in (yp, ym, xx):
        pl.semaphore_signal(free, inc=1, device_id={"tensor": to}, device_id_type=MESH)

    part = KV.at[pl.ds(mo((1 - c) * 512, 512), 512), 0 : 2 * HEAD]
    send(part, part, kv_s.at[0], kv_r.at[0], other).wait_recv()

    def attend(r, head):
        rows, columns = pl.ds(mo(r * 16, 16), 16), pl.ds(mo(head * HEAD, HEAD), HEAD)
        query = Q[:, rows, columns].reshape(128, HEAD)
        scores = lax.dot_general(
            query, KV[:, 0:HEAD], (((1,), (1,)), ((), ())), preferred_element_type=F32
        )
        end = E[:, pl.ds(mo(c * 64 + r * 16, 16), 16), 0:1].reshape(128, 1)
        scores = jnp.where(KID[0:1, :] < end, scores, -1e30 * HEAD**0.5)
        top = jnp.max(scores, axis=-1, keepdims=True)
        expo = jnp.exp2((scores - top) * (LOG2E / HEAD**0.5)).astype(BF)
        mixed = jnp.dot(expo, KV[:, HEAD : 3 * HEAD], preferred_element_type=F32)
        CTX[lax.rem(r, 2), :, columns] = (mixed[:, :HEAD] / mixed[:, HEAD:]).astype(BF)

    def attend_first(head, carry):
        attend(0, head)
        return carry

    lax.fori_loop(0, 8, attend_first, 0)
    pl.semaphore_wait(free, 3)
    for q in range(4):
        wo_local(q).wait()
        part = WO.at[q, pl.ds(mo((1 - c) * 512, 512), 512), :]
        send(part, part, wo_s.at[q], wo_r.at[q], other).wait_recv()

    def arrived(kind, k):
        into, at = {6: (5, 1), 7: (6, 0)}.get(kind, (kind, 0))
        o, line = slot(k, into, at)
        part = G.at[o, pl.ds(line, 16 if kind in (5, 6) else 32), :]
        send(part, part, rs_s.at[kind, k], rs_r.at[kind, k], xx).wait_recv()

    def reduce_step(i, carry):
        k1, k2, k3 = i - SKEW, i - 2 * SKEW, i - 3 * SKEW

        @pl.when(i < 16)
        def _():
            r, q = lax.div(i, 4), lax.rem(i, 4)
            for half in range(2):
                terms = jnp.dot(
                    CTX[lax.rem(r, 2)],
                    WO[q, :, half * 1024 : (half + 1) * 1024],
                    preferred_element_type=F32,
                ).astype(BF)
                for b in range(8):
                    n, row = term(i, b, half)
                    WQ[n, pl.ds(row, 16), :] = terms[b * 16 : (b + 1) * 16]
            reduce(7, i).start()
            reduce(3, i).start()
            reduce(4, i).start()

        @pl.when((k1 >= 0) & (k1 < 16))
        def _():
            arrived(7, k1)
            for half in range(2):
                add_in(k1, block(2, 0), half, [(6, half)])
                reduce(5 + half, k1).start()

            @pl.when(jnp.logical_not(across(k1)))
            def _():
                arrived(3, k1)
                arrived(4, k1)
                for half in range(2):
                    add_in(k1, block(0, 1), half, [(3, half), (4, half)])

            reduce(2, k1).start()

        @pl.when((k2 >= 0) & (k2 < 16))
        def _():
            arrived(5, k2)
            add_in(k2, block(3, 0), 0, [(5, 0)])
            arrived(6, k2)
            add_in(k2, block(1, 0), 1, [(5, 1)])

            @pl.when(across(k2))
            def _():
                arrived(3, k2)
                arrived(4, k2)
                for half in range(2):
                    add_in(k2, block(3, 0), half, [(3, half)])
                    add_in(k2, block(1, 0), half, [(4, half)])

            reduce(0, k2).start()
            reduce(1, k2).start()

        @pl.when(k3 >= 0)
        def _():
            for kind in range(3):
                arrived(kind, k3)
            r, q = lax.div(k3, 4), lax.rem(k3, 4)
            rows = pl.ds(mo(r * 16, 16), 16)
            for half in range(2):
                total, _, _ = add(k3, own, half, [(0, half), (1, half), (2, half)])
                columns = pl.ds(mo(q * 2048 + half * 1024, 1024), 1024)
                STG[rows, columns] = (hid[0, rows, columns].astype(F32) + total).astype(BF)
            hand(k3).start()

        @pl.when(i < 12)
        def _():
            for n in range(2):
                attend(lax.div(i, 4) + 1, lax.rem(i, 4) * 2 + n)

        return carry

    lax.fori_loop(0, 16 + 3 * SKEW, reduce_step, 0)

    def sent(k, carry):
        for kind in range(8):
            reduce(kind, k).wait_send()
        hand(k).wait()
        return carry

    lax.fori_loop(0, 16, sent, 0)
    for d in range(1, 8):
        for n, w in enumerate((wk, wv)):
            kvw(w, n, d).wait_send()
    for d in range(8):
        forward(d).wait_send()
    for j in range(8):
        wq_push(j).wait_send()
    for q in range(4):
        wo_push(q).wait_send()
    bias_push.wait_send()
    part = KV.at[pl.ds(mo(c * 512, 512), 512), 0 : 2 * HEAD]
    send(part, part, kv_s.at[0], kv_r.at[0], other).wait_send()


def on_device(
    hidden_in, norm_gain, w_query, bias_query, w_key, w_value, bias_value, w_out, visible_end
):
    vmem, anywhere = pl.BlockSpec(memory_space=pltpu.VMEM), pl.BlockSpec(memory_space=pl.ANY)
    dma = pltpu.SemaphoreType.DMA
    return pl.pallas_call(
        layer,
        out_shape=jax.ShapeDtypeStruct(hidden_in.shape, BF),
        in_specs=[vmem, vmem, anywhere, vmem, anywhere, anywhere, vmem, anywhere, vmem],
        out_specs=anywhere,
        scratch_shapes=[
            pltpu.VMEM((8, 512, 1024), BF),
            pltpu.VMEM((8, 1024, 1024), BF),
            pltpu.VMEM((8, 1024, 256), BF),
            pltpu.VMEM((4, 1024, 2048), BF),
            pltpu.VMEM((512, 1024), F32),
            pltpu.VMEM((512, 256), F32),
            pltpu.VMEM((8, 64, 1024), BF),
            pltpu.VMEM((1024, 384), BF),
            pltpu.VMEM((2, 128, 1024), BF),
            pltpu.VMEM((2, 16, 512), BF),
            pltpu.VMEM((8, 128, 128), F32),
            pltpu.VMEM((8, 1024), F32),
            pltpu.VMEM((64, 8192), BF),
            dma((8, 8)), dma((8, 8)), dma((8, 16)), dma((8, 16)), dma((16,)), dma((16,)),
            dma((2, 8)), dma((2, 8)), dma((2,)), dma((8,)), dma((8,)),
            dma((8,)), dma((8,)), dma((8,)), dma((4,)), dma((4,)), dma((4,)),
            dma((1,)), dma((1,)), dma((1,)), dma((1,)), pltpu.SemaphoreType.REGULAR,
        ],
        compiler_params=pltpu.CompilerParams(
            collective_id=0, has_side_effects=True, vmem_limit_bytes=63 * 2**20
        ),
        cost_estimate=pl.CostEstimate(flops=24 * 10**9, bytes_accessed=40 * 10**6, transcendentals=4 * 2**20),
    )(
        hidden_in, norm_gain, w_query, bias_query, w_key, w_value, bias_value, w_out, visible_end
    )


def solution(mesh):
    placed = (
        P("section", "tensor", None),
        P("section", None),
        P("section", None, "tensor"),
        P("section", "tensor"),
        P("section", "tensor", None),
        P("section", "tensor", None),
        P("section", None),
        P("section", "tensor", None),
        P("section", None),
    )
    return jax.shard_map(
        on_device,
        mesh=mesh,
        in_specs=placed,
        out_specs=P("section", "tensor", None),
        check_vma=False,
    )
```

time: 424 us -> 182 us (0.43)
  waiting for transfers between devices: 306 us -> 0 us
  Pallas kernels: 0 us -> 179 us
  matrix products: 59.2 us -> 0 us
  local copies, waits for them, and re-layouts: 20.9 us -> 2.26 us
  other arithmetic: 15.4 us -> 0 us
  between operations: 13.6 us -> 0.01 us
  starting transfers between devices: 8.84 us -> 0 us
    pallas_call x0 -> x1, Pallas kernels: none -> 179 us  [on_device(): pl.pallas_call(layer, out_shape=jax.ShapeDtypeStruct(hidden_in.shape, BF)...]
    reduce_scatter x1 -> x0, waiting for transfers between devices: 145 us -> none  [on_device(): lax.psum_scatter(jnp.dot(context, out_rows, preferred_element_type=jnp.fl...]
    all_gather x1 -> x0, waiting for transfers between devices: 70.4 us -> none  [on_device(): normed = normalize(lax.all_gather(rows, 'tensor', axis=0, tiled=True), gain)]
    all_to_all x1 -> x0, waiting for transfers between devices: 64.4 us -> none  [on_device(): lax.all_to_all(spread, 'tensor', split_axis=2, concat_axis=0, tiled=True)]
    dot_general x4 -> x0, matrix products: 49.6 us -> none  [the longest x1 15.8 us: on_device(): jnp.dot(context, out_rows, preferred_element_type=jnp.float32)]
    ppermute x1 -> x0, waiting for transfers between devices: 24.8 us -> none  [from_behind(): lax.ppermute(array, axis, [(i, (i + by) % count) for i in range(count)])]
    unnamed x17 -> x1, local copies, waits for them, and re-layouts: 12.8 us -> 2.26 us
    sub x1 -> x0, matrix products: 9.61 us -> none  [on_device(): expo = jnp.exp(scores - top)]
  transfers between devices with their start and end apart: 4 -> 0, of which waited for: 4 -> 0; matrix products, arithmetic and copies ran while one was open for 3% -> 0% of each run, Pallas kernels for 0% -> 0%
where the time goes in v1:
time: 182 us; the launch traced here: 181 us
  Pallas kernels  179 us (98%)
  local copies, waits for them, and re-layouts  2.26 us (1%)
    pallas_call x1, Pallas kernels, on_device(): pl.pallas_call(layer, out_shape=jax.ShapeDtypeStruct(hidden_in.shape, BF)...  179 us

profile of v1, /device:TPU:0, one launch (start us, length us, event | category | flops | bytes accessed | tf_op | source)
XLA Modules:
  0.0 181.0 jit_solution(7785216226377117154)
XLA Ops:
  0.0 178.8 %shard_map.91 = bf16[1,64,8192]{2,1,0:T(8,128)(2,1)} custom-call(bf16[1,64,8192]{2,1,0:T(8,128)(2,1)} %hid.1, bf16[1,8192]{1,0:T(2,128)(2,1)} %gain.1, bf16[1,8192,512]{2,1,0:T(8,128)(2,1)} %wq.1, bf16[1,512]{1,0:T(2,128)(2,1)} %bq.1, bf16[1,512,1024]{2,1,0:T(8,128)(2,1)} %wk.1, bf16[1,512,1024]{2,1,0:T(8,128)(2,1)} %wv.1, bf16[1,1024]{1,0:T(2,128)(2,1)} %bv.1, ...), custom_call_target="tpu_custom_call" | custom-call | flops 24000000000 | bytes 40000000 | tf_op jit(solution)/shard_map/pallas_call | solution.py:465
  178.8 2.3 %copy.11 = bf16[1,64,8192]{2,1,0:T(8,128)(2,1)} copy(bf16[1,64,8192]{2,1,0:T(8,128)(2,1)} %shard_map.91) | data formatting | bytes 2097152

commit v2 on v0

v2 whole, which is shorter than its diff:
```python
import jax
import jax.numpy as jnp
from jax import lax
from jax.experimental import pallas as pl
from jax.experimental.pallas import tpu as pltpu
from jax.sharding import PartitionSpec as P

MESH = pl.DeviceIdType.MESH
BF = jnp.bfloat16
F32 = jnp.float32
HEAD = 128
RELAYED = 4
UP_FRONT = 4
KV_STEPS = (2, 5, 4)
LOG2E = 1.4426950408889634


def mo(value, by):
    return pl.multiple_of(value, by)


def layer(
    hid, gain, wq, bq, wk, wv, bv, wo, ends, out,
    G, WQ, WKV, WO, ACC, KVT, KVIN, Q, KV, CTX, BQ, E, KID, STG, RELAY,
    ag_s, ag_r, rs_s, rs_r, ho_s, ho_r, rl_s, rl_r, wkv_l, wkv_s, wkv_r, kvt_s, kvt_r,
    wq_l, wq_s, wq_r, wo_l, wo_s, wo_r, bq_s, bq_r, kv_s, kv_r, free,
):
    section = lax.axis_index("section")
    place = lax.axis_index("tensor")
    y, h, c = lax.div(place, 4), lax.rem(lax.div(place, 2), 2), lax.rem(place, 2)
    chip = lax.div(place, 2)

    def block(dy, flip):
        return lax.rem(y + dy, 4) * 2 + (1 - h if flip else h)

    def peer(dy, flip):
        return block(dy, flip) * 2 + c

    yp, ym, xx = peer(1, 0), peer(3, 0), peer(0, 1)
    other = chip * 2 + (1 - c)
    own = chip
    nxt, prv = lax.rem(section + 1, 8), lax.rem(section + 7, 8)
    half, z = lax.div(section, 4), lax.rem(section, 4)
    first, last = z == 0, z == 3

    def send(src, dst, ss, rs, to):
        return pltpu.make_async_remote_copy(
            src_ref=src, dst_ref=dst, send_sem=ss, recv_sem=rs,
            device_id={"tensor": to}, device_id_type=MESH,
        )

    def wq_local(j):
        return pltpu.make_async_copy(
            wq.at[0, pl.ds(mo(j * 1024, 1024), 1024), :],
            WQ.at[j, :, pl.ds(mo(c * 512, 512), 512)],
            wq_l.at[j],
        )

    def wo_local(q):
        return pltpu.make_async_copy(
            wo.at[0, :, pl.ds(mo(q * 1024, 1024), 1024)],
            WO.at[q, pl.ds(mo(c * 512, 512), 512), :],
            wo_l.at[q],
        )

    def kv_local(w, n):
        return pltpu.make_async_copy(
            w.at[0], WKV.at[n, pl.ds(mo(c * 512, 512), 512), :], wkv_l.at[n]
        )

    def kv_push(w, n):
        there = WKV.at[n, pl.ds(mo(c * 512, 512), 512), :]
        return send(w.at[0], there, wkv_s.at[n], wkv_r.at[n], other)

    def wq_push(j):
        return send(
            wq.at[0, pl.ds(mo(j * 1024, 1024), 1024), :],
            WQ.at[j, :, pl.ds(mo(c * 512, 512), 512)],
            wq_s.at[j], wq_r.at[j], other,
        )

    def wo_push(q):
        return send(
            wo.at[0, :, pl.ds(mo(q * 1024, 1024), 1024)],
            WO.at[q, pl.ds(mo(c * 512, 512), 512), :],
            wo_s.at[q], wo_r.at[q], other,
        )

    def piece(b, j, lo=0, n=64):
        return G.at[j, pl.ds(mo(b * 64 + lo, 32), n), :]

    def gather(kind, j):
        b = (own, own, own, block(0, 1), block(0, 1), block(3, 0), block(1, 0), block(2, 0))[kind]
        to = (yp, ym, xx, yp, ym, yp, ym, xx)[kind]
        part = piece(b, j, 32 if kind == 6 else 0, 32 if kind in (5, 6) else 64)
        return send(part, part, ag_s.at[kind, j], ag_r.at[kind, j], to)

    def gather_side(kind):
        b = block(3, 0) if kind == 3 else block(1, 0)
        part = piece(b, b)
        return send(part, part, ag_s.at[kind, block(0, 1)], ag_r.at[kind, b], xx)

    def gathered(kind, j):
        b = (block(3, 0), block(1, 0), block(0, 1), block(3, 1), block(1, 1),
             block(2, 0), block(2, 0), block(2, 1))[kind]
        part = piece(b, j, 32 if kind == 6 else 0, 32 if kind in (5, 6) else 64)
        send(part, part, ag_s.at[kind, j], ag_r.at[kind, j], xx).wait_recv()

    def kv_sum(kind):
        b = (block(3, 0), block(1, 0), block(0, 1), block(3, 1), block(1, 1),
             block(2, 0), block(2, 0), block(2, 1))[kind]
        lo, n = (256 if kind == 6 else 0), (256 if kind in (5, 6) else 512)
        to = (ym, yp, xx, ym, yp, ym, yp, xx)[kind]
        into = (0, 1, 2, 3, 4, 5, 5, 6)[kind]
        return send(
            KVT.at[b, lo : lo + n, :], KVIN.at[into, lo : lo + n, :],
            kvt_s.at[kind], kvt_r.at[kind], to,
        )

    def kv_came(kind):
        lo, n = (256 if kind == 6 else 0), (256 if kind in (5, 6) else 512)
        into = (0, 1, 2, 3, 4, 5, 5, 6)[kind]
        part = KVIN.at[into, lo : lo + n, :]
        send(part, part, kvt_s.at[kind], kvt_r.at[kind], xx).wait_recv()
        return KVIN[into, lo : lo + n, :].astype(F32)

    order = (
        block(2, 1), block(1, 1), block(3, 1), block(2, 0), block(0, 1), block(1, 0), block(3, 0), own,
    )

    def reduce(kind, k):
        at, n = (384, 320, 256, 128, 64, 192, 224, 0)[kind], 32 if kind in (5, 6) else 64
        line = (0, 64, 128, 192, 256, 320, 352, 384)[kind]
        to = (ym, yp, xx, ym, yp, ym, yp, xx)[kind]
        return send(
            WQ.at[k, at : at + n, :], G.at[k, line : line + n, :],
            rs_s.at[kind, k], rs_r.at[kind, k], to,
        )

    def arrived(kind, k):
        n = 32 if kind in (5, 6) else 64
        line = (0, 64, 128, 192, 256, 320, 352, 384)[kind]
        part = G.at[k, line : line + n, :]
        send(part, part, rs_s.at[kind, k], rs_r.at[kind, k], xx).wait_recv()
        return G[k, line : line + n, :].astype(F32)

    def term(k, at, n=64):
        return WQ[k, at : at + n, :].astype(F32)

    def hand_to(src, dst, ss, rs, to):
        return pltpu.make_async_remote_copy(
            src_ref=src, dst_ref=dst, send_sem=ss, recv_sem=rs,
            device_id={"section": to}, device_id_type=MESH,
        )

    def hand(k):
        columns = pl.ds(mo(k * 1024, 1024), 1024)
        return hand_to(STG.at[:, columns], out.at[0, :, columns], ho_s.at[k], ho_r.at[k], nxt)

    def relay_in(k):
        columns = pl.ds(mo(k * 1024, 1024), 1024)
        return hand_to(STG.at[:, columns], RELAY.at[k], ho_s.at[k], rl_r.at[k], half * 4)

    def relay_out(k):
        columns = pl.ds(mo(k * 1024, 1024), 1024)
        to = (1 - half) * 4
        return hand_to(RELAY.at[k], out.at[0, :, columns], rl_s.at[k], ho_r.at[k], to)

    for n, w in enumerate((wk, wv)):
        kv_local(w, n).start()
    for j in range(8):
        wq_local(j).start()
    for q in range(8):
        wo_local(q).start()

    barrier = pltpu.get_barrier_semaphore()
    for to in (yp, ym, xx, other):
        pl.semaphore_signal(barrier, inc=1, device_id={"tensor": to}, device_id_type=MESH)
    pl.semaphore_signal(barrier, inc=1, device_id={"section": prv}, device_id_type=MESH)

    @pl.when(first)
    def _():
        for to in (half * 4 + 3, (1 - half) * 4):
            pl.semaphore_signal(barrier, inc=1, device_id={"section": to}, device_id_type=MESH)

    @pl.when(first | last)
    def _():
        pl.semaphore_wait(barrier, 6)

    @pl.when(jnp.logical_not(first | last))
    def _():
        pl.semaphore_wait(barrier, 5)


    for n, w in enumerate((wk, wv)):
        kv_push(w, n).start()

    def norm_rows(rg, carry):
        rows = hid[0, pl.ds(mo(rg * 16, 16), 16), :].astype(F32)
        power = jnp.mean(rows * rows, axis=-1, keepdims=True)
        scale = lax.rsqrt(power + 1e-06)
        normed = (rows * scale * gain[...].astype(F32)).astype(BF)
        for j in range(8):
            G[j, pl.ds(mo(own * 64 + rg * 16, 16), 16), :] = normed[:, j * 1024 : (j + 1) * 1024]
        return carry

    lax.fori_loop(0, 4, norm_rows, 0)
    rest = [block(0, 0), block(0, 1), block(1, 1), block(3, 1)]
    own_order = (
        [block(1, 0), block(2, 0), block(2, 1), block(3, 0), *rest],
        [block(3, 0), block(2, 0), block(2, 1), block(1, 0), *rest],
        [block(0, 1), block(1, 1), block(3, 1), block(2, 1), block(0, 0), block(1, 0), block(2, 0), block(3, 0)],
    )
    for n in range(UP_FRONT):
        for kind in range(3):
            gather(kind, own_order[kind][n]).start()
    BQ[c] = jnp.broadcast_to(bq[...], (16, 512))
    bias_push = send(BQ.at[c], BQ.at[c], bq_s.at[0], bq_r.at[0], other)
    bias_push.start()
    for j in range(8):
        wq_push(j).start()
    for q in range(8):
        wo_push(q).start()
    ACC[...] = jnp.zeros_like(ACC)
    for b in range(8):
        line = jnp.broadcast_to(ends[:, b * 128 : (b + 1) * 128].astype(F32), (128, 128))
        E[b] = line.T
    lane = lax.broadcasted_iota(jnp.int32, (8, 512), 1)
    token = lane + lax.div(lane, 64) * 64
    KID[:, 0:512] = token.astype(F32)
    KID[:, 512:1024] = (token + 64).astype(F32)
    KV[:, 256:384] = jnp.ones((1024, 128), BF)

    gathered(0, block(1, 0))
    gather(5, block(1, 0)).start()
    gathered(1, block(3, 0))
    gather(6, block(3, 0)).start()
    gathered(2, block(1, 0))
    gather(3, block(1, 0)).start()
    gathered(2, block(3, 0))
    gather(4, block(3, 0)).start()
    gathered(0, block(1, 1))
    gather(5, block(1, 1)).start()
    gathered(1, block(3, 1))
    gather(6, block(3, 1)).start()
    for n in range(UP_FRONT, 8):
        for kind in range(3):
            gather(kind, own_order[kind][n]).start()
    gathered(5, block(0, 1))
    gathered(6, block(0, 1))
    gather(7, block(0, 1)).start()
    gathered(0, own)
    gather(5, own).start()
    gathered(1, own)
    gather(6, own).start()
    for kind in range(2, 8):
        gathered(kind, own)

    for n, w in enumerate((wk, wv)):
        kv_local(w, n).wait()
        part = WKV.at[n, pl.ds(mo((1 - c) * 512, 512), 512), :]
        send(part, part, wkv_s.at[n], wkv_r.at[n], other).wait_recv()
        for m in range(2):
            sums = jnp.dot(
                G[own], WKV[n, :, m * 512 : (m + 1) * 512], preferred_element_type=F32
            ).astype(BF)
            for b in range(4):
                KVT[m * 4 + b, :, n * HEAD : (n + 1) * HEAD] = sums[:, b * HEAD : (b + 1) * HEAD]
    for kind in (7, 3, 4):
        kv_sum(kind).start()

    def pass_along(j, carry):
        @pl.when((j != block(1, 0)) & (j != block(1, 1)) & (j != own))
        def _():
            gathered(0, j)
            gather(5, j).start()

        @pl.when((j != block(3, 0)) & (j != block(3, 1)) & (j != own))
        def _():
            gathered(1, j)
            gather(6, j).start()

        return carry

    lax.fori_loop(0, 8, pass_along, 0)
    gather_side(3).start()
    gather_side(4).start()

    def pass_across(j, carry):
        @pl.when((j != block(1, 0)) & (j != block(3, 0)) & (j != own))
        def _():
            gathered(2, j)

        @pl.when((j != block(1, 0)) & (j != block(0, 1)))
        def _():
            gather(3, j).start()

        @pl.when((j != block(3, 0)) & (j != block(0, 1)))
        def _():
            gather(4, j).start()

        @pl.when(j != block(0, 1))
        def _():
            @pl.when(j != own)
            def _():
                gathered(5, j)
                gathered(6, j)

            gather(7, j).start()

        @pl.when(j == KV_STEPS[0])
        def _():
            b = block(2, 0)
            KVT[b] = (KVT[b].astype(F32) + kv_came(7)).astype(BF)
            kv_sum(5).start()
            kv_sum(6).start()
            b = block(0, 1)
            KVT[b] = (KVT[b].astype(F32) + kv_came(3) + kv_came(4)).astype(BF)
            kv_sum(2).start()

        @pl.when(j == KV_STEPS[1])
        def _():
            b = block(3, 0)
            KVT[b, 0:256, :] = (KVT[b, 0:256, :].astype(F32) + kv_came(5)).astype(BF)
            kv_sum(0).start()
            b = block(1, 0)
            KVT[b, 256:512, :] = (KVT[b, 256:512, :].astype(F32) + kv_came(6)).astype(BF)
            kv_sum(1).start()

        return carry

    lax.fori_loop(0, 8, pass_across, 0)

    def project(j, carry):
        wq_local(j).wait()
        part = WQ.at[j, :, pl.ds(mo((1 - c) * 512, 512), 512)]
        send(part, part, wq_s.at[j], wq_r.at[j], other).wait_recv()

        @pl.when(j != own)
        def _():
            gathered(3, j)
            gathered(4, j)
            gathered(7, j)

        for n in range(2):
            columns = slice(n * 512, (n + 1) * 512)
            ACC[:, columns] += jnp.dot(G[j], WQ[j, :, columns], preferred_element_type=F32)

        @pl.when(j == KV_STEPS[2])
        def _():
            total = KVT[own].astype(F32) + kv_came(0) + kv_came(1) + kv_came(2)
            rows = pl.ds(mo(c * 512, 512), 512)
            KV[rows, 0:HEAD] = total[:, 0:HEAD].astype(BF)
            bias = bv[:, pl.ds(mo(chip * HEAD, HEAD), HEAD)].astype(F32)
            KV[rows, HEAD : 2 * HEAD] = (total[:, HEAD:] + bias).astype(BF)
            part = KV.at[rows, 0 : 2 * HEAD]
            send(part, part, kv_s.at[0], kv_r.at[0], other).start()

        return carry

    lax.fori_loop(0, 8, project, 0)

    send(BQ.at[1 - c], BQ.at[1 - c], bq_s.at[0], bq_r.at[0], other).wait_recv()
    for n in range(2):
        for b in range(8):
            Q[b, :, n * 512 : (n + 1) * 512] = (
                ACC[b * 64 : (b + 1) * 64, n * 512 : (n + 1) * 512] + BQ[n, 0:1, :].astype(F32)
            ).astype(BF)

    def gather_sent(j, carry):
        for kind in range(8):
            gather(kind, j).wait_send()
        return carry

    lax.fori_loop(0, 8, gather_sent, 0)
    for to in (yp, ym, xx):
        pl.semaphore_signal(free, inc=1, device_id={"tensor": to}, device_id_type=MESH)

    part = KV.at[pl.ds(mo((1 - c) * 512, 512), 512), 0 : 2 * HEAD]
    send(part, part, kv_s.at[0], kv_r.at[0], other).wait_recv()

    def attend(first, last, head):
        columns = pl.ds(mo(head * HEAD, HEAD), HEAD)
        blocks = order[first:last]
        query = jnp.concatenate([Q[b, :, columns] for b in blocks], axis=0)
        scores = lax.dot_general(
            query, KV[:, 0:HEAD], (((1,), (1,)), ((), ())), preferred_element_type=F32
        )
        end = jnp.concatenate([E[b, pl.ds(mo(c * 64, 64), 64), 0:1] for b in blocks], axis=0)
        scores = jnp.where(KID[0:1, :] < end, scores, -1e30 * HEAD**0.5)
        top = jnp.max(scores, axis=-1, keepdims=True)
        expo = jnp.exp2((scores - top) * (LOG2E / HEAD**0.5)).astype(BF)
        mixed = jnp.dot(expo, KV[:, HEAD : 3 * HEAD], preferred_element_type=F32)
        CTX[first * 64 : last * 64, columns] = (mixed[:, :HEAD] / mixed[:, HEAD:]).astype(BF)

    def terms(first, last, k):
        rows = slice(first * 64, last * 64)
        WQ[k, rows, :] = jnp.dot(CTX[rows, :], WO[k], preferred_element_type=F32).astype(BF)

    def attend_first(head, carry):
        attend(0, 3, head)
        return carry

    lax.fori_loop(0, 8, attend_first, 0)
    pl.semaphore_wait(free, 3)

    def far_terms(k, carry):
        wo_local(k).wait()
        part = WO.at[k, pl.ds(mo((1 - c) * 512, 512), 512), :]
        send(part, part, wo_s.at[k], wo_r.at[k], other).wait_recv()
        terms(0, 3, k)
        reduce(3, k).start()
        reduce(4, k).start()
        reduce(7, k).start()
        attend(3, 5, k)
        return carry

    lax.fori_loop(0, 8, far_terms, 0)

    def middle_terms(k, carry):
        terms(3, 5, k)
        WQ[k, 192:256, :] = (term(k, 192) + arrived(7, k)).astype(BF)
        reduce(5, k).start()
        reduce(6, k).start()
        WQ[k, 256:320, :] = (term(k, 256) + arrived(3, k) + arrived(4, k)).astype(BF)
        reduce(2, k).start()
        attend(5, 8, k)
        return carry

    lax.fori_loop(0, 8, middle_terms, 0)

    def near_terms(i, carry):
        @pl.when(i < 8)
        def _():
            k = i
            terms(5, 8, k)
            WQ[k, 384:416, :] = (term(k, 384, 32) + arrived(5, k)).astype(BF)
            WQ[k, 352:384, :] = (term(k, 352, 32) + arrived(6, k)).astype(BF)
            reduce(0, k).start()
            reduce(1, k).start()

        @pl.when(i >= 1)
        def _():
            k = i - 1
            columns = pl.ds(mo(k * 1024, 1024), 1024)
            total = term(k, 448) + arrived(0, k) + arrived(1, k) + arrived(2, k)
            STG[:, columns] = (hid[0, :, columns].astype(F32) + total).astype(BF)

            @pl.when(last & (k < RELAYED))
            def _():
                relay_in(k).start()

            @pl.when(jnp.logical_not(last & (k < RELAYED)))
            def _():
                hand(k).start()

        @pl.when(first & (i >= 3) & (i < 3 + RELAYED))
        def _():
            relay_in(i - 3).wait_recv()
            relay_out(i - 3).start()

        return carry

    lax.fori_loop(0, 9, near_terms, 0)

    def sent(k, carry):
        for kind in range(8):
            reduce(kind, k).wait_send()
        hand(k).wait()

        @pl.when(first & (k < RELAYED))
        def _():
            relay_out(k).wait_send()

        return carry

    lax.fori_loop(0, 8, sent, 0)
    for n, w in enumerate((wk, wv)):
        kv_push(w, n).wait_send()
    for kind in range(8):
        kv_sum(kind).wait_send()
    for j in range(8):
        wq_push(j).wait_send()
    for q in range(8):
        wo_push(q).wait_send()
    bias_push.wait_send()
    part = KV.at[pl.ds(mo(c * 512, 512), 512), 0 : 2 * HEAD]
    send(part, part, kv_s.at[0], kv_r.at[0], other).wait_send()


def on_device(
    hidden_in, norm_gain, w_query, bias_query, w_key, w_value, bias_value, w_out, visible_end
):
    vmem, anywhere = pl.BlockSpec(memory_space=pltpu.VMEM), pl.BlockSpec(memory_space=pl.ANY)
    dma = pltpu.SemaphoreType.DMA
    return pl.pallas_call(
        layer,
        out_shape=jax.ShapeDtypeStruct(hidden_in.shape, BF),
        in_specs=[vmem, vmem, anywhere, vmem, anywhere, anywhere, vmem, anywhere, vmem],
        out_specs=anywhere,
        scratch_shapes=[
            pltpu.VMEM((8, 512, 1024), BF),
            pltpu.VMEM((8, 1024, 1024), BF),
            pltpu.VMEM((2, 1024, 1024), BF),
            pltpu.VMEM((8, 1024, 1024), BF),
            pltpu.VMEM((512, 1024), F32),
            pltpu.VMEM((8, 512, 256), BF),
            pltpu.VMEM((7, 512, 256), BF),
            pltpu.VMEM((8, 64, 1024), BF),
            pltpu.VMEM((1024, 384), BF),
            pltpu.VMEM((512, 1024), BF),
            pltpu.VMEM((2, 16, 512), BF),
            pltpu.VMEM((8, 128, 128), F32),
            pltpu.VMEM((8, 1024), F32),
            pltpu.VMEM((64, 8192), BF),
            pltpu.VMEM((RELAYED, 64, 1024), BF),
            dma((8, 8)), dma((8, 8)), dma((8, 8)), dma((8, 8)), dma((8,)), dma((8,)), dma((8,)), dma((8,)),
            dma((2,)), dma((2,)), dma((2,)), dma((8,)), dma((8,)),
            dma((8,)), dma((8,)), dma((8,)), dma((8,)), dma((8,)), dma((8,)),
            dma((1,)), dma((1,)), dma((1,)), dma((1,)), pltpu.SemaphoreType.REGULAR,
        ],
        compiler_params=pltpu.CompilerParams(
            collective_id=0, has_side_effects=True, vmem_limit_bytes=63 * 2**20
        ),
        cost_estimate=pl.CostEstimate(flops=24 * 10**9, bytes_accessed=40 * 10**6, transcendentals=4 * 2**20),
    )(
        hidden_in, norm_gain, w_query, bias_query, w_key, w_value, bias_value, w_out, visible_end
    )


def solution(mesh):
    placed = (
        P("section", "tensor", None),
        P("section", None),
        P("section", None, "tensor"),
        P("section", "tensor"),
        P("section", "tensor", None),
        P("section", "tensor", None),
        P("section", None),
        P("section", "tensor", None),
        P("section", None),
    )
    return jax.shard_map(
        on_device,
        mesh=mesh,
        in_specs=placed,
        out_specs=P("section", "tensor", None),
        check_vma=False,
    )
```

time: 424 us -> 159 us (0.38)
  waiting for transfers between devices: 306 us -> 0 us
  Pallas kernels: 0 us -> 156 us
  matrix products: 59.2 us -> 0 us
  local copies, waits for them, and re-layouts: 20.9 us -> 2.26 us
  other arithmetic: 15.4 us -> 0 us
  between operations: 13.6 us -> 0.01 us
  starting transfers between devices: 8.84 us -> 0 us
    pallas_call x0 -> x1, Pallas kernels: none -> 156 us  [on_device(): pl.pallas_call(layer, out_shape=jax.ShapeDtypeStruct(hidden_in.shape, BF)...]
    reduce_scatter x1 -> x0, waiting for transfers between devices: 145 us -> none  [on_device(): lax.psum_scatter(jnp.dot(context, out_rows, preferred_element_type=jnp.fl...]
    all_gather x1 -> x0, waiting for transfers between devices: 70.4 us -> none  [on_device(): normed = normalize(lax.all_gather(rows, 'tensor', axis=0, tiled=True), gain)]
    all_to_all x1 -> x0, waiting for transfers between devices: 64.4 us -> none  [on_device(): lax.all_to_all(spread, 'tensor', split_axis=2, concat_axis=0, tiled=True)]
    dot_general x4 -> x0, matrix products: 49.6 us -> none  [the longest x1 15.8 us: on_device(): jnp.dot(context, out_rows, preferred_element_type=jnp.float32)]
    ppermute x1 -> x0, waiting for transfers between devices: 24.8 us -> none  [from_behind(): lax.ppermute(array, axis, [(i, (i + by) % count) for i in range(count)])]
    unnamed x17 -> x1, local copies, waits for them, and re-layouts: 12.8 us -> 2.26 us
    sub x1 -> x0, matrix products: 9.61 us -> none  [on_device(): expo = jnp.exp(scores - top)]
  transfers between devices with their start and end apart: 4 -> 0, of which waited for: 4 -> 0; matrix products, arithmetic and copies ran while one was open for 3% -> 0% of each run, Pallas kernels for 0% -> 0%
where the time goes in v2:
time: 159 us; the launch traced here: 158 us
  Pallas kernels  156 us (98%)
  local copies, waits for them, and re-layouts  2.26 us (1%)
    pallas_call x1, Pallas kernels, on_device(): pl.pallas_call(layer, out_shape=jax.ShapeDtypeStruct(hidden_in.shape, BF)...  156 us

profile of v2, /device:TPU:0, one launch (start us, length us, event | category | flops | bytes accessed | tf_op | source)
XLA Modules:
  0.0 158.4 jit_solution(3600455176825991639)
XLA Ops:
  0.0 156.2 %shard_map.91 = bf16[1,64,8192]{2,1,0:T(8,128)(2,1)} custom-call(bf16[1,64,8192]{2,1,0:T(8,128)(2,1)} %hid.1, bf16[1,8192]{1,0:T(2,128)(2,1)} %gain.1, bf16[1,8192,512]{2,1,0:T(8,128)(2,1)} %wq.1, bf16[1,512]{1,0:T(2,128)(2,1)} %bq.1, bf16[1,512,1024]{2,1,0:T(8,128)(2,1)} %wk.1, bf16[1,512,1024]{2,1,0:T(8,128)(2,1)} %wv.1, bf16[1,1024]{1,0:T(2,128)(2,1)} %bv.1, ...), custom_call_target="tpu_custom_call" | custom-call | flops 24000000000 | bytes 40000000 | tf_op jit(solution)/shard_map/pallas_call | solution.py:496
  156.2 2.3 %copy.11 = bf16[1,64,8192]{2,1,0:T(8,128)(2,1)} copy(bf16[1,64,8192]{2,1,0:T(8,128)(2,1)} %shard_map.91) | data formatting | bytes 2097152

commit v3 on v2

--- a/solution.py
+++ b/solution.py
@@ -10,8 +10,10 @@
 F32 = jnp.float32
 HEAD = 128
 RELAYED = 4
-UP_FRONT = 4
+UP_FRONT = (4, 4, 6)
 KV_STEPS = (2, 5, 4)
+FIRST = 2
+STEPS = (2, 4, 5, 7)
 LOG2E = 1.4426950408889634
 
 
@@ -20,9 +22,9 @@
 
 
 def layer(
-    hid, gain, wq, bq, wk, wv, bv, wo, ends, out,
-    G, WQ, WKV, WO, ACC, KVT, KVIN, Q, KV, CTX, BQ, E, KID, STG, RELAY,
-    ag_s, ag_r, rs_s, rs_r, ho_s, ho_r, rl_s, rl_r, wkv_l, wkv_s, wkv_r, kvt_s, kvt_r,
+    hidden, gain, wq, bq, wk, wv, bv, wo, ends, out,
+    G, WQ, WKV, WO, ACC, KVT, KVIN, Q, KV, CTX, BQ, E, END, KID, HID, STG, RELAY,
+    ag_s, ag_r, rs_s, rs_r, ho_s, ho_r, rl_s, rl_r, hid_l, wkv_l, wkv_s, wkv_r, kvt_s, kvt_r,
     wq_l, wq_s, wq_r, wo_l, wo_s, wo_r, bq_s, bq_r, kv_s, kv_r, free,
 ):
     section = lax.axis_index("section")
@@ -125,24 +127,24 @@
         return KVIN[into, lo : lo + n, :].astype(F32)
 
     order = (
-        block(2, 1), block(1, 1), block(3, 1), block(2, 0), block(0, 1), block(1, 0), block(3, 0), own,
+        block(1, 1), block(3, 1), block(2, 1), block(2, 0), block(0, 1), block(1, 0), block(3, 0), own,
     )
 
+    def lands(kind, k):
+        line, n = (0, 64, 128, 192, 256, 320, 352, 384)[kind], 32 if kind in (5, 6) else 64
+        return G.at[k, line : line + n, :]
+
     def reduce(kind, k):
-        at, n = (384, 320, 256, 128, 64, 192, 224, 0)[kind], 32 if kind in (5, 6) else 64
-        line = (0, 64, 128, 192, 256, 320, 352, 384)[kind]
+        at, n = (384, 320, 256, 64, 0, 192, 224, 128)[kind], 32 if kind in (5, 6) else 64
         to = (ym, yp, xx, ym, yp, ym, yp, xx)[kind]
         return send(
-            WQ.at[k, at : at + n, :], G.at[k, line : line + n, :],
-            rs_s.at[kind, k], rs_r.at[kind, k], to,
+            WQ.at[k, at : at + n, :], lands(kind, k), rs_s.at[kind, k], rs_r.at[kind, k], to
         )
 
     def arrived(kind, k):
-        n = 32 if kind in (5, 6) else 64
-        line = (0, 64, 128, 192, 256, 320, 352, 384)[kind]
-        part = G.at[k, line : line + n, :]
+        part = lands(kind, k)
         send(part, part, rs_s.at[kind, k], rs_r.at[kind, k], xx).wait_recv()
-        return G[k, line : line + n, :].astype(F32)
+        return part[...].astype(F32)
 
     def term(k, at, n=64):
         return WQ[k, at : at + n, :].astype(F32)
@@ -166,6 +168,8 @@
         to = (1 - half) * 4
         return hand_to(RELAY.at[k], out.at[0, :, columns], rl_s.at[k], ho_r.at[k], to)
 
+    hid_copy = pltpu.make_async_copy(hidden.at[0], HID, hid_l.at[0])
+    hid_copy.start()
     for n, w in enumerate((wk, wv)):
         kv_local(w, n).start()
     for j in range(8):
@@ -196,7 +200,7 @@
         kv_push(w, n).start()
 
     def norm_rows(rg, carry):
-        rows = hid[0, pl.ds(mo(rg * 16, 16), 16), :].astype(F32)
+        rows = HID[pl.ds(mo(rg * 16, 16), 16), :].astype(F32)
         power = jnp.mean(rows * rows, axis=-1, keepdims=True)
         scale = lax.rsqrt(power + 1e-06)
         normed = (rows * scale * gain[...].astype(F32)).astype(BF)
@@ -204,6 +208,7 @@
             G[j, pl.ds(mo(own * 64 + rg * 16, 16), 16), :] = normed[:, j * 1024 : (j + 1) * 1024]
         return carry
 
+    hid_copy.wait()
     lax.fori_loop(0, 4, norm_rows, 0)
     rest = [block(0, 0), block(0, 1), block(1, 1), block(3, 1)]
     own_order = (
@@ -211,9 +216,10 @@
         [block(3, 0), block(2, 0), block(2, 1), block(1, 0), *rest],
         [block(0, 1), block(1, 1), block(3, 1), block(2, 1), block(0, 0), block(1, 0), block(2, 0), block(3, 0)],
     )
-    for n in range(UP_FRONT):
+    for n in range(8):
         for kind in range(3):
-            gather(kind, own_order[kind][n]).start()
+            if n < UP_FRONT[kind]:
+                gather(kind, own_order[kind][n]).start()
     BQ[c] = jnp.broadcast_to(bq[...], (16, 512))
     bias_push = send(BQ.at[c], BQ.at[c], bq_s.at[0], bq_r.at[0], other)
     bias_push.start()
@@ -230,6 +236,23 @@
     KID[:, 0:512] = token.astype(F32)
     KID[:, 512:1024] = (token + 64).astype(F32)
     KV[:, 256:384] = jnp.ones((1024, 128), BF)
+    for n, b in enumerate(order):
+        END[n * 64 : (n + 1) * 64, :] = E[b, pl.ds(mo(c * 64, 64), 64), :]
+
+    def project(first, last, j):
+        rows = slice(first * 64, last * 64)
+        normed = jnp.concatenate(
+            [G[j, pl.ds(mo(b * 64, 64), 64), :] for b in order[first:last]], axis=0
+        )
+        for n in range(2):
+            columns = slice(n * 512, (n + 1) * 512)
+            ACC[rows, columns] += jnp.dot(normed, WQ[j, :, columns], preferred_element_type=F32)
+
+    def queries(first, last):
+        rows = slice(first * 64, last * 64)
+        for n in range(2):
+            columns = slice(n * 512, (n + 1) * 512)
+            Q[rows, columns] = (ACC[rows, columns] + BQ[n, 0:1, :].astype(F32)).astype(BF)
 
     gathered(0, block(1, 0))
     gather(5, block(1, 0)).start()
@@ -243,12 +266,15 @@
     gather(5, block(1, 1)).start()
     gathered(1, block(3, 1))
     gather(6, block(3, 1)).start()
-    for n in range(UP_FRONT, 8):
-        for kind in range(3):
-            gather(kind, own_order[kind][n]).start()
+    for n in range(8):
+        for kind in range(2):
+            if n >= UP_FRONT[kind]:
+                gather(kind, own_order[kind][n]).start()
     gathered(5, block(0, 1))
     gathered(6, block(0, 1))
     gather(7, block(0, 1)).start()
+    for n in range(UP_FRONT[2], 8):
+        gather(2, own_order[2][n]).start()
     gathered(0, own)
     gather(5, own).start()
     gathered(1, own)
@@ -327,24 +353,27 @@
             KVT[b, 256:512, :] = (KVT[b, 256:512, :].astype(F32) + kv_came(6)).astype(BF)
             kv_sum(1).start()
 
-        return carry
-
-    lax.fori_loop(0, 8, pass_across, 0)
-
-    def project(j, carry):
         wq_local(j).wait()
         part = WQ.at[j, :, pl.ds(mo((1 - c) * 512, 512), 512)]
         send(part, part, wq_s.at[j], wq_r.at[j], other).wait_recv()
+        project(4, 8, j)
+        return carry
+
+    lax.fori_loop(0, 8, pass_across, 0)
+
+    def project_far(j, carry):
+        @pl.when(j != own)
+        def _():
+            gathered(7, j)
+
+        project(2, 4, j)
 
         @pl.when(j != own)
         def _():
             gathered(3, j)
             gathered(4, j)
-            gathered(7, j)
-
-        for n in range(2):
-            columns = slice(n * 512, (n + 1) * 512)
-            ACC[:, columns] += jnp.dot(G[j], WQ[j, :, columns], preferred_element_type=F32)
+
+        project(0, 2, j)
 
         @pl.when(j == KV_STEPS[2])
         def _():
@@ -358,14 +387,7 @@
 
         return carry
 
-    lax.fori_loop(0, 8, project, 0)
-
-    send(BQ.at[1 - c], BQ.at[1 - c], bq_s.at[0], bq_r.at[0], other).wait_recv()
-    for n in range(2):
-        for b in range(8):
-            Q[b, :, n * 512 : (n + 1) * 512] = (
-                ACC[b * 64 : (b + 1) * 64, n * 512 : (n + 1) * 512] + BQ[n, 0:1, :].astype(F32)
-            ).astype(BF)
+    lax.fori_loop(0, 8, project_far, 0)
 
     def gather_sent(j, carry):
         for kind in range(8):
@@ -375,93 +397,115 @@
     lax.fori_loop(0, 8, gather_sent, 0)
     for to in (yp, ym, xx):
         pl.semaphore_signal(free, inc=1, device_id={"tensor": to}, device_id_type=MESH)
-
+    send(BQ.at[1 - c], BQ.at[1 - c], bq_s.at[0], bq_r.at[0], other).wait_recv()
+    queries(0, 2)
     part = KV.at[pl.ds(mo((1 - c) * 512, 512), 512), 0 : 2 * HEAD]
     send(part, part, kv_s.at[0], kv_r.at[0], other).wait_recv()
 
-    def attend(first, last, head):
-        columns = pl.ds(mo(head * HEAD, HEAD), HEAD)
-        blocks = order[first:last]
-        query = jnp.concatenate([Q[b, :, columns] for b in blocks], axis=0)
+    def attend(first, last, head, heads):
+        rows = slice(first * 64, last * 64)
+        columns = [pl.ds(mo((head + n) * HEAD, HEAD), HEAD) for n in range(heads)]
+        query = jnp.concatenate([Q[rows, at] for at in columns], axis=0)
+        end = jnp.concatenate([END[rows, 0:1]] * heads, axis=0)
         scores = lax.dot_general(
             query, KV[:, 0:HEAD], (((1,), (1,)), ((), ())), preferred_element_type=F32
         )
-        end = jnp.concatenate([E[b, pl.ds(mo(c * 64, 64), 64), 0:1] for b in blocks], axis=0)
         scores = jnp.where(KID[0:1, :] < end, scores, -1e30 * HEAD**0.5)
         top = jnp.max(scores, axis=-1, keepdims=True)
         expo = jnp.exp2((scores - top) * (LOG2E / HEAD**0.5)).astype(BF)
         mixed = jnp.dot(expo, KV[:, HEAD : 3 * HEAD], preferred_element_type=F32)
-        CTX[first * 64 : last * 64, columns] = (mixed[:, :HEAD] / mixed[:, HEAD:]).astype(BF)
+        mixed = (mixed[:, :HEAD] / mixed[:, HEAD:]).astype(BF)
+        count = (last - first) * 64
+        for n, at in enumerate(columns):
+            CTX[rows, at] = mixed[n * count : (n + 1) * count]
 
     def terms(first, last, k):
         rows = slice(first * 64, last * 64)
         WQ[k, rows, :] = jnp.dot(CTX[rows, :], WO[k], preferred_element_type=F32).astype(BF)
 
-    def attend_first(head, carry):
-        attend(0, 3, head)
-        return carry
-
-    lax.fori_loop(0, 8, attend_first, 0)
-    pl.semaphore_wait(free, 3)
-
-    def far_terms(k, carry):
+    def attend_two(first):
+        def pair_of(pair, carry):
+            attend(first, first + 2, pair * 2, 2)
+            return carry
+
+        lax.fori_loop(0, 4, pair_of, 0)
+
+    def side(k):
         wo_local(k).wait()
         part = WO.at[k, pl.ds(mo((1 - c) * 512, 512), 512), :]
         send(part, part, wo_s.at[k], wo_r.at[k], other).wait_recv()
-        terms(0, 3, k)
+        terms(0, 2, k)
         reduce(3, k).start()
         reduce(4, k).start()
-        reduce(7, k).start()
-        attend(3, 5, k)
-        return carry
-
-    lax.fori_loop(0, 8, far_terms, 0)
-
-    def middle_terms(k, carry):
-        terms(3, 5, k)
+
+    attend_two(0)
+    pl.semaphore_wait(free, 3)
+    for k in range(FIRST):
+        side(k)
+    queries(2, 8)
+    attend_two(2)
+
+    def step(i, carry):
+        @pl.when(i < 8)
+        def _():
+            terms(2, 4, i)
+            reduce(7, i).start()
+
+        @pl.when(i < 8 - FIRST)
+        def _():
+            side(i + FIRST)
+
+        @pl.when(i < 4)
+        def _():
+            attend(4, 8, 2 * i, 1)
+            attend(4, 8, 2 * i + 1, 1)
+
+        def at(steps, work):
+            @pl.when((i >= steps) & (i < 8 + steps))
+            def _():
+                work(i - steps)
+
+        at(STEPS[0], opposite)
+        at(STEPS[1], across)
+        at(STEPS[2], near)
+        at(STEPS[3], finish)
+        return carry
+
+    def opposite(k):
         WQ[k, 192:256, :] = (term(k, 192) + arrived(7, k)).astype(BF)
         reduce(5, k).start()
         reduce(6, k).start()
+
+    def across(k):
+        terms(4, 8, k)
         WQ[k, 256:320, :] = (term(k, 256) + arrived(3, k) + arrived(4, k)).astype(BF)
         reduce(2, k).start()
-        attend(5, 8, k)
-        return carry
-
-    lax.fori_loop(0, 8, middle_terms, 0)
-
-    def near_terms(i, carry):
-        @pl.when(i < 8)
-        def _():
-            k = i
-            terms(5, 8, k)
-            WQ[k, 384:416, :] = (term(k, 384, 32) + arrived(5, k)).astype(BF)
-            WQ[k, 352:384, :] = (term(k, 352, 32) + arrived(6, k)).astype(BF)
-            reduce(0, k).start()
-            reduce(1, k).start()
-
-        @pl.when(i >= 1)
-        def _():
-            k = i - 1
-            columns = pl.ds(mo(k * 1024, 1024), 1024)
-            total = term(k, 448) + arrived(0, k) + arrived(1, k) + arrived(2, k)
-            STG[:, columns] = (hid[0, :, columns].astype(F32) + total).astype(BF)
-
-            @pl.when(last & (k < RELAYED))
-            def _():
-                relay_in(k).start()
-
-            @pl.when(jnp.logical_not(last & (k < RELAYED)))
-            def _():
-                hand(k).start()
-
-        @pl.when(first & (i >= 3) & (i < 3 + RELAYED))
-        def _():
-            relay_in(i - 3).wait_recv()
-            relay_out(i - 3).start()
-
-        return carry
-
-    lax.fori_loop(0, 9, near_terms, 0)
+
+    def near(k):
+        WQ[k, 384:416, :] = (term(k, 384, 32) + arrived(5, k)).astype(BF)
+        reduce(0, k).start()
+        WQ[k, 352:384, :] = (term(k, 352, 32) + arrived(6, k)).astype(BF)
+        reduce(1, k).start()
+
+    def finish(k):
+        columns = pl.ds(mo(k * 1024, 1024), 1024)
+        total = term(k, 448) + arrived(0, k) + arrived(1, k) + arrived(2, k)
+        STG[:, columns] = (HID[:, columns].astype(F32) + total).astype(BF)
+
+        @pl.when(last & (k < RELAYED))
+        def _():
+            relay_in(k).start()
+
+        @pl.when(jnp.logical_not(last & (k < RELAYED)))
+        def _():
+            hand(k).start()
+
+        @pl.when(first & (k >= 2) & (k < 2 + RELAYED))
+        def _():
+            relay_in(k - 2).wait_recv()
+            relay_out(k - 2).start()
+
+    lax.fori_loop(0, 8 + STEPS[3], step, 0)
 
     def sent(k, carry):
         for kind in range(8):
@@ -496,7 +540,7 @@
     return pl.pallas_call(
         layer,
         out_shape=jax.ShapeDtypeStruct(hidden_in.shape, BF),
-        in_specs=[vmem, vmem, anywhere, vmem, anywhere, anywhere, vmem, anywhere, vmem],
+        in_specs=[anywhere, vmem, anywhere, vmem, anywhere, anywhere, vmem, anywhere, vmem],
         out_specs=anywhere,
         scratch_shapes=[
             pltpu.VMEM((8, 512, 1024), BF),
@@ -506,16 +550,18 @@
             pltpu.VMEM((512, 1024), F32),
             pltpu.VMEM((8, 512, 256), BF),
             pltpu.VMEM((7, 512, 256), BF),
-            pltpu.VMEM((8, 64, 1024), BF),
+            pltpu.VMEM((512, 1024), BF),
             pltpu.VMEM((1024, 384), BF),
             pltpu.VMEM((512, 1024), BF),
             pltpu.VMEM((2, 16, 512), BF),
             pltpu.VMEM((8, 128, 128), F32),
+            pltpu.VMEM((512, 128), F32),
             pltpu.VMEM((8, 1024), F32),
+            pltpu.VMEM((64, 8192), BF),
             pltpu.VMEM((64, 8192), BF),
             pltpu.VMEM((RELAYED, 64, 1024), BF),
             dma((8, 8)), dma((8, 8)), dma((8, 8)), dma((8, 8)), dma((8,)), dma((8,)), dma((8,)), dma((8,)),
-            dma((2,)), dma((2,)), dma((2,)), dma((8,)), dma((8,)),
+            dma((1,)), dma((2,)), dma((2,)), dma((2,)), dma((8,)), dma((8,)),
             dma((8,)), dma((8,)), dma((8,)), dma((8,)), dma((8,)), dma((8,)),
             dma((1,)), dma((1,)), dma((1,)), dma((1,)), pltpu.SemaphoreType.REGULAR,
         ],

time: 159 us -> 156 us (0.981)
  Pallas kernels: 156 us -> 153 us
    pallas_call x1, Pallas kernels: 156 us -> 153 us  [on_device(): pl.pallas_call(layer, out_shape=jax.ShapeDtypeStruct(hidden_in.shape, BF)...]
where the time goes in v3:
time: 156 us; the launch traced here: 155 us
  Pallas kernels  153 us (98%)
  local copies, waits for them, and re-layouts  2.26 us (1%)
    pallas_call x1, Pallas kernels, on_device(): pl.pallas_call(layer, out_shape=jax.ShapeDtypeStruct(hidden_in.shape, BF)...  153 us

profile of v3, /device:TPU:0, one launch (start us, length us, event | category | flops | bytes accessed | tf_op | source)
XLA Modules:
  0.0 155.5 jit_solution(5975750036023677173)
XLA Ops:
  0.0 153.2 %shard_map.91 = bf16[1,64,8192]{2,1,0:T(8,128)(2,1)} custom-call(bf16[1,64,8192]{2,1,0:T(8,128)(2,1)} %hidden.1, bf16[1,8192]{1,0:T(2,128)(2,1)} %gain.1, bf16[1,8192,512]{2,1,0:T(8,128)(2,1)} %wq.1, bf16[1,512]{1,0:T(2,128)(2,1)} %bq.1, bf16[1,512,1024]{2,1,0:T(8,128)(2,1)} %wk.1, bf16[1,512,1024]{2,1,0:T(8,128)(2,1)} %wv.1, bf16[1,1024]{1,0:T(2,128)(2,1)} %bv.1, ...), custom_call_target="tpu_custom_call" | custom-call | flops 24000000000 | bytes 40000000 | tf_op jit(solution)/shard_map/pallas_call | solution.py:540
  153.2 2.3 %copy.11 = bf16[1,64,8192]{2,1,0:T(8,128)(2,1)} copy(bf16[1,64,8192]{2,1,0:T(8,128)(2,1)} %shard_map.91) | data formatting | bytes 2097152

commit v4 on v3

--- a/solution.py
+++ b/solution.py
@@ -14,6 +14,7 @@
 KV_STEPS = (2, 5, 4)
 FIRST = 2
 STEPS = (2, 4, 5, 7)
+STACK = 4
 LOG2E = 1.4426950408889634
 
 
@@ -170,34 +171,22 @@
 
     hid_copy = pltpu.make_async_copy(hidden.at[0], HID, hid_l.at[0])
     hid_copy.start()
+    barrier = pltpu.get_barrier_semaphore()
+    for to in (yp, ym, xx, other):
+        pl.semaphore_signal(barrier, inc=1, device_id={"tensor": to}, device_id_type=MESH)
+    pl.semaphore_signal(barrier, inc=1, device_id={"section": prv}, device_id_type=MESH)
+
+    @pl.when(first)
+    def _():
+        for to in (half * 4 + 3, (1 - half) * 4):
+            pl.semaphore_signal(barrier, inc=1, device_id={"section": to}, device_id_type=MESH)
+
     for n, w in enumerate((wk, wv)):
         kv_local(w, n).start()
     for j in range(8):
         wq_local(j).start()
     for q in range(8):
         wo_local(q).start()
-
-    barrier = pltpu.get_barrier_semaphore()
-    for to in (yp, ym, xx, other):
-        pl.semaphore_signal(barrier, inc=1, device_id={"tensor": to}, device_id_type=MESH)
-    pl.semaphore_signal(barrier, inc=1, device_id={"section": prv}, device_id_type=MESH)
-
-    @pl.when(first)
-    def _():
-        for to in (half * 4 + 3, (1 - half) * 4):
-            pl.semaphore_signal(barrier, inc=1, device_id={"section": to}, device_id_type=MESH)
-
-    @pl.when(first | last)
-    def _():
-        pl.semaphore_wait(barrier, 6)
-
-    @pl.when(jnp.logical_not(first | last))
-    def _():
-        pl.semaphore_wait(barrier, 5)
-
-
-    for n, w in enumerate((wk, wv)):
-        kv_push(w, n).start()
 
     def norm_rows(rg, carry):
         rows = HID[pl.ds(mo(rg * 16, 16), 16), :].astype(F32)
@@ -210,6 +199,19 @@
 
     hid_copy.wait()
     lax.fori_loop(0, 4, norm_rows, 0)
+
+    @pl.when(first | last)
+    def _():
+        pl.semaphore_wait(barrier, 6)
+
+    @pl.when(jnp.logical_not(first | last))
+    def _():
+        pl.semaphore_wait(barrier, 5)
+
+
+    for n, w in enumerate((wk, wv)):
+        kv_push(w, n).start()
+
     rest = [block(0, 0), block(0, 1), block(1, 1), block(3, 1)]
     own_order = (
         [block(1, 0), block(2, 0), block(2, 1), block(3, 0), *rest],
@@ -374,6 +376,8 @@
             gathered(4, j)
 
         project(0, 2, j)
+        for kind in range(8):
+            gather(kind, j).wait_send()
 
         @pl.when(j == KV_STEPS[2])
         def _():
@@ -389,12 +393,6 @@
 
     lax.fori_loop(0, 8, project_far, 0)
 
-    def gather_sent(j, carry):
-        for kind in range(8):
-            gather(kind, j).wait_send()
-        return carry
-
-    lax.fori_loop(0, 8, gather_sent, 0)
     for to in (yp, ym, xx):
         pl.semaphore_signal(free, inc=1, device_id={"tensor": to}, device_id_type=MESH)
     send(BQ.at[1 - c], BQ.at[1 - c], bq_s.at[0], bq_r.at[0], other).wait_recv()
@@ -424,11 +422,11 @@
         WQ[k, rows, :] = jnp.dot(CTX[rows, :], WO[k], preferred_element_type=F32).astype(BF)
 
     def attend_two(first):
-        def pair_of(pair, carry):
-            attend(first, first + 2, pair * 2, 2)
+        def group(n, carry):
+            attend(first, first + 2, n * STACK, STACK)
             return carry
 
-        lax.fori_loop(0, 4, pair_of, 0)
+        lax.fori_loop(0, 8 // STACK, group, 0)
 
     def side(k):
         wo_local(k).wait()
@@ -457,8 +455,7 @@
 
         @pl.when(i < 4)
         def _():
-            attend(4, 8, 2 * i, 1)
-            attend(4, 8, 2 * i + 1, 1)
+            attend(4, 8, 2 * i, 2)
 
         def at(steps, work):
             @pl.when((i >= steps) & (i < 8 + steps))
@@ -510,7 +507,7 @@
     def sent(k, carry):
         for kind in range(8):
             reduce(kind, k).wait_send()
-        hand(k).wait()
+        hand(k).wait_send()
 
         @pl.when(first & (k < RELAYED))
         def _():
@@ -530,6 +527,13 @@
     bias_push.wait_send()
     part = KV.at[pl.ds(mo(c * 512, 512), 512), 0 : 2 * HEAD]
     send(part, part, kv_s.at[0], kv_r.at[0], other).wait_send()
+
+
+    def handed(k, carry):
+        hand(k).wait_recv()
+        return carry
+
+    lax.fori_loop(0, 8, handed, 0)
 
 
 def on_device(

time: 156 us -> 150 us (0.962)
  Pallas kernels: 153 us -> 148 us
    pallas_call x1, Pallas kernels: 153 us -> 148 us  [on_device(): pl.pallas_call(layer, out_shape=jax.ShapeDtypeStruct(hidden_in.shape, BF)...]
where the time goes in v4:
time: 150 us
  Pallas kernels  148 us (99%)
  local copies, waits for them, and re-layouts  2.26 us (2%)
    pallas_call x1, Pallas kernels, on_device(): pl.pallas_call(layer, out_shape=jax.ShapeDtypeStruct(hidden_in.shape, BF)...  148 us

profile of v4, /device:TPU:0, one launch (start us, length us, event | category | flops | bytes accessed | tf_op | source)
XLA Modules:
  0.0 150.0 jit_solution(17731124161700567026)
XLA Ops:
  0.0 147.7 %shard_map.91 = bf16[1,64,8192]{2,1,0:T(8,128)(2,1)} custom-call(bf16[1,64,8192]{2,1,0:T(8,128)(2,1)} %hidden.1, bf16[1,8192]{1,0:T(2,128)(2,1)} %gain.1, bf16[1,8192,512]{2,1,0:T(8,128)(2,1)} %wq.1, bf16[1,512]{1,0:T(2,128)(2,1)} %bq.1, bf16[1,512,1024]{2,1,0:T(8,128)(2,1)} %wk.1, bf16[1,512,1024]{2,1,0:T(8,128)(2,1)} %wv.1, bf16[1,1024]{1,0:T(2,128)(2,1)} %bv.1, ...), custom_call_target="tpu_custom_call" | custom-call | flops 24000000000 | bytes 40000000 | tf_op jit(solution)/shard_map/pallas_call | solution.py:544
  147.7 2.3 %copy.11 = bf16[1,64,8192]{2,1,0:T(8,128)(2,1)} copy(bf16[1,64,8192]{2,1,0:T(8,128)(2,1)} %shard_map.91) | data formatting | bytes 2097152

commit v5 on v4

--- a/solution.py
+++ b/solution.py
@@ -25,7 +25,7 @@
 def layer(
     hidden, gain, wq, bq, wk, wv, bv, wo, ends, out,
     G, WQ, WKV, WO, ACC, KVT, KVIN, Q, KV, CTX, BQ, E, END, KID, HID, STG, RELAY,
-    ag_s, ag_r, rs_s, rs_r, ho_s, ho_r, rl_s, rl_r, hid_l, wkv_l, wkv_s, wkv_r, kvt_s, kvt_r,
+    ag_s, ag_r, rs_s, rs_r, ho_s, ho_r, rl_s, rl_r, hs_s, hs_r, hid_l, wkv_l, wkv_s, wkv_r, kvt_s, kvt_r,
     wq_l, wq_s, wq_r, wo_l, wo_s, wo_r, bq_s, bq_r, kv_s, kv_r, free,
 ):
     section = lax.axis_index("section")
@@ -102,6 +102,30 @@
         b = block(3, 0) if kind == 3 else block(1, 0)
         part = piece(b, b)
         return send(part, part, ag_s.at[kind, block(0, 1)], ag_r.at[kind, b], xx)
+
+    def gather_half(kind):
+        j = block(2, 1)
+        part = piece(block(0, 1), j, 0, 32)
+        return send(part, part, ag_s.at[kind, j], ag_r.at[kind, j], yp if kind == 3 else ym)
+
+    def gather_half_side(kind):
+        b, j = (block(3, 0), block(1, 0)) if kind == 3 else (block(1, 0), block(3, 0))
+        part = piece(b, j, 32, 32)
+        return send(part, part, hs_s.at[kind - 3], hs_r.at[kind - 3], xx)
+
+    def gathered_side(kind, j):
+        b, halved = (block(3, 1), block(1, 1)) if kind == 3 else (block(1, 1), block(3, 1))
+
+        @pl.when(j != halved)
+        def _():
+            gathered(kind, j)
+
+        @pl.when(j == halved)
+        def _():
+            part = piece(b, j, 0, 32)
+            send(part, part, ag_s.at[kind, j], ag_r.at[kind, j], xx).wait_recv()
+            part = piece(b, j, 32, 32)
+            send(part, part, hs_s.at[kind - 3], hs_r.at[kind - 3], xx).wait_recv()
 
     def gathered(kind, j):
         b = (block(3, 0), block(1, 0), block(0, 1), block(3, 1), block(1, 1),
@@ -313,19 +337,26 @@
     lax.fori_loop(0, 8, pass_along, 0)
     gather_side(3).start()
     gather_side(4).start()
+    gather_half_side(3).start()
+    gather_half_side(4).start()
 
     def pass_across(j, carry):
         @pl.when((j != block(1, 0)) & (j != block(3, 0)) & (j != own))
         def _():
             gathered(2, j)
 
-        @pl.when((j != block(1, 0)) & (j != block(0, 1)))
+        @pl.when((j != block(1, 0)) & (j != block(0, 1)) & (j != block(2, 1)))
         def _():
             gather(3, j).start()
 
-        @pl.when((j != block(3, 0)) & (j != block(0, 1)))
+        @pl.when((j != block(3, 0)) & (j != block(0, 1)) & (j != block(2, 1)))
         def _():
             gather(4, j).start()
+
+        @pl.when(j == block(2, 1))
+        def _():
+            gather_half(3).start()
+            gather_half(4).start()
 
         @pl.when(j != block(0, 1))
         def _():
@@ -372,12 +403,23 @@
 
         @pl.when(j != own)
         def _():
-            gathered(3, j)
-            gathered(4, j)
+            gathered_side(3, j)
+            gathered_side(4, j)
 
         project(0, 2, j)
-        for kind in range(8):
+        for kind in (0, 1, 2, 5, 6, 7):
             gather(kind, j).wait_send()
+
+        @pl.when(j != block(2, 1))
+        def _():
+            gather(3, j).wait_send()
+            gather(4, j).wait_send()
+
+        @pl.when(j == block(2, 1))
+        def _():
+            for kind in (3, 4):
+                gather_half(kind).wait_send()
+                gather_half_side(kind).wait_send()
 
         @pl.when(j == KV_STEPS[2])
         def _():
@@ -565,6 +607,7 @@
             pltpu.VMEM((64, 8192), BF),
             pltpu.VMEM((RELAYED, 64, 1024), BF),
             dma((8, 8)), dma((8, 8)), dma((8, 8)), dma((8, 8)), dma((8,)), dma((8,)), dma((8,)), dma((8,)),
+            dma((2,)), dma((2,)),
             dma((1,)), dma((2,)), dma((2,)), dma((2,)), dma((8,)), dma((8,)),
             dma((8,)), dma((8,)), dma((8,)), dma((8,)), dma((8,)), dma((8,)),
             dma((1,)), dma((1,)), dma((1,)), dma((1,)), pltpu.SemaphoreType.REGULAR,

time: 150 us -> 149 us (level)
  no operation moved by 1% of the time
where the time goes in v5:
time: 149 us
  Pallas kernels  147 us (99%)
  local copies, waits for them, and re-layouts  2.26 us (2%)
    pallas_call x1, Pallas kernels, on_device(): pl.pallas_call(layer, out_shape=jax.ShapeDtypeStruct(hidden_in.shape, BF)...  147 us

profile of v5, /device:TPU:0, one launch (start us, length us, event | category | flops | bytes accessed | tf_op | source)
XLA Modules:
  0.0 148.9 jit_solution(14985710283136473272)
XLA Ops:
  0.0 146.6 %shard_map.91 = bf16[1,64,8192]{2,1,0:T(8,128)(2,1)} custom-call(bf16[1,64,8192]{2,1,0:T(8,128)(2,1)} %hidden.1, bf16[1,8192]{1,0:T(2,128)(2,1)} %gain.1, bf16[1,8192,512]{2,1,0:T(8,128)(2,1)} %wq.1, bf16[1,512]{1,0:T(2,128)(2,1)} %bq.1, bf16[1,512,1024]{2,1,0:T(8,128)(2,1)} %wk.1, bf16[1,512,1024]{2,1,0:T(8,128)(2,1)} %wv.1, bf16[1,1024]{1,0:T(2,128)(2,1)} %bv.1, ...), custom_call_target="tpu_custom_call" | custom-call | flops 24000000000 | bytes 40000000 | tf_op jit(solution)/shard_map/pallas_call | solution.py:586
  146.6 2.3 %copy.11 = bf16[1,64,8192]{2,1,0:T(8,128)(2,1)} copy(bf16[1,64,8192]{2,1,0:T(8,128)(2,1)} %shard_map.91) | data formatting | bytes 2097152

commit v6 on v5

--- a/solution.py
+++ b/solution.py
@@ -12,7 +12,7 @@
 RELAYED = 4
 UP_FRONT = (4, 4, 6)
 KV_STEPS = (2, 5, 4)
-FIRST = 2
+FIRST = 1
 STEPS = (2, 4, 5, 7)
 STACK = 4
 LOG2E = 1.4426950408889634
@@ -233,9 +233,6 @@
         pl.semaphore_wait(barrier, 5)
 
 
-    for n, w in enumerate((wk, wv)):
-        kv_push(w, n).start()
-
     rest = [block(0, 0), block(0, 1), block(1, 1), block(3, 1)]
     own_order = (
         [block(1, 0), block(2, 0), block(2, 1), block(3, 0), *rest],
@@ -246,6 +243,8 @@
         for kind in range(3):
             if n < UP_FRONT[kind]:
                 gather(kind, own_order[kind][n]).start()
+    for n, w in enumerate((wk, wv)):
+        kv_push(w, n).start()
     BQ[c] = jnp.broadcast_to(bq[...], (16, 512))
     bias_push = send(BQ.at[c], BQ.at[c], bq_s.at[0], bq_r.at[0], other)
     bias_push.start()

time: 149 us -> 151 us (1.013)
    pallas_call x1, Pallas kernels: 147 us -> 148 us  [on_device(): pl.pallas_call(layer, out_shape=jax.ShapeDtypeStruct(hidden_in.shape, BF)...]
where the time goes in v6:
time: 151 us
  Pallas kernels  148 us (98%)
  local copies, waits for them, and re-layouts  2.26 us (1%)
    pallas_call x1, Pallas kernels, on_device(): pl.pallas_call(layer, out_shape=jax.ShapeDtypeStruct(hidden_in.shape, BF)...  148 us

profile of v6, /device:TPU:0, one launch (start us, length us, event | category | flops | bytes accessed | tf_op | source)
XLA Modules:
  0.0 150.6 jit_solution(4967208854896639679)
XLA Ops:
  0.0 148.3 %shard_map.91 = bf16[1,64,8192]{2,1,0:T(8,128)(2,1)} custom-call(bf16[1,64,8192]{2,1,0:T(8,128)(2,1)} %hidden.1, bf16[1,8192]{1,0:T(2,128)(2,1)} %gain.1, bf16[1,8192,512]{2,1,0:T(8,128)(2,1)} %wq.1, bf16[1,512]{1,0:T(2,128)(2,1)} %bq.1, bf16[1,512,1024]{2,1,0:T(8,128)(2,1)} %wk.1, bf16[1,512,1024]{2,1,0:T(8,128)(2,1)} %wv.1, bf16[1,1024]{1,0:T(2,128)(2,1)} %bv.1, ...), custom_call_target="tpu_custom_call" | custom-call | flops 24000000000 | bytes 40000000 | tf_op jit(solution)/shard_map/pallas_call | solution.py:585
  148.3 2.3 %copy.11 = bf16[1,64,8192]{2,1,0:T(8,128)(2,1)} copy(bf16[1,64,8192]{2,1,0:T(8,128)(2,1)} %shard_map.91) | data formatting | bytes 2097152
